TPU v7x, 32 devices: a whole 2x2x4 slice. The times are simulated.
32 devices in a mesh: gz: 8 (over z, y), ky: 4 (over x, core).
Axes of the slice: x: 2, y: 2, z: 4, core: 2. Of those that a mesh axis runs over, the one named last changes fastest.
Arguments:
- fields: bfloat16 [256, 3, 2, 32768], P('gz', None, None, 'ky'), may hold values from -6 to 6
- wall_operator: bfloat16 [256, 256], replicated, may hold values from -0.375 to 0.375
- remap_offset: int32 [4, 4], replicated, may hold values from 0 to 31, as said below
- remap_count: int32 [4, 4], replicated, may hold values from 1 to 8, as said below
Outputs:
- spectra: float32 [256, 3, 2, 32768], P('gz', None, None, 'ky')
Inputs may be any that keep to these rules, and one draw needn't show every extreme that they name: remap_count[g, h] rows go from group g to group h; in every draw one group h receives exactly 8 rows from every group. The run from group g to group h is rows remap_offset[g, h] to remap_offset[g, h] + remap_count[g, h] - 1 of group g's 32 rows; the runs of one group do not intersect.
All inputs are finite; a program needn't handle non-finite values.
Results may differ from a plain program's by a relative error of at most 0.0048.
Values may be sent and summed in bfloat16 or wider, within the bound.
No kernel may reach another device: no remote copies, remote signals or barrier semaphores. Data moves between devices by JAX's collectives and lax.ppermute only.
A program may use at most 128 MiB of HBM per device.

v0:
```python
import functools
import math

import jax
import jax.numpy as jnp
import ml_dtypes
import numpy as np
from jax import lax
from jax.experimental import pallas as pl
from jax.experimental.pallas import tpu as pltpu
from jax.sharding import PartitionSpec as P

NU_COEF = 0.05
STEP_DT = 0.3
SLOT = 8
LANES = 128
FLIPS = (2, 0)
SENDERS = (0, 2, 1, 3)
BF16 = jnp.bfloat16
F32 = jnp.float32
PARAMS = pltpu.CompilerParams(vmem_limit_bytes=56 * 2**20)


def mode_matrix(half_z):
    row = np.arange(half_z)[:, None]
    column = np.arange(half_z)[None, :]
    norm = math.sqrt(2.0 / half_z)
    step = math.pi / (2 * half_z)
    cosine = norm * np.cos(((row * (2 * column + 1)) % (4 * half_z)) * step)
    sine = norm * np.sin((((row + 1) * (2 * (half_z - 1 - column) + 1)) % (4 * half_z)) * step)
    cosine = cosine.astype(np.float32).astype(ml_dtypes.bfloat16).astype(np.float32)
    sine = sine.astype(np.float32).astype(ml_dtypes.bfloat16).astype(np.float32)
    top = np.concatenate([0.5 * cosine, 0.5 * cosine[:, ::-1]], axis=1)
    bottom = np.concatenate([0.5 * sine[:, ::-1], -0.5 * sine], axis=1)
    whole = np.concatenate([top, bottom], axis=0)
    return np.kron(whole, np.eye(2, dtype=np.float32)).astype(ml_dtypes.bfloat16)


def mode_factors(half_z):
    index = np.arange(2 * half_z)
    wave = np.where(index < half_z, index, index - half_z + 1) * (math.pi / half_z)
    pair = np.stack([np.exp(-NU_COEF * wave * wave), STEP_DT * wave]).astype(np.float32)
    return np.broadcast_to(np.repeat(pair, 2, axis=1)[:, :, None], (2, 4 * half_z, LANES)).copy()


def sent_runs(count, group, flip):
    first = count[group, group ^ flip]
    return first, first + count[group, group ^ flip ^ 1]


def choose(count, sizes):
    def body(count_ref, out_ref):
        choice = 0
        for flip in FLIPS:
            most = 0
            for group in range(4):
                most = jnp.maximum(most, sent_runs(count_ref, group, flip)[1])
            choice = choice * len(sizes) + sum((most > size).astype(jnp.int32) for size in sizes[:-1])
        out_ref[0] = choice

    smem = pl.BlockSpec(memory_space=pltpu.SMEM)
    return pl.pallas_call(
        body, in_specs=[smem], out_specs=smem, out_shape=jax.ShapeDtypeStruct((1,), jnp.int32)
    )(count)[0]


def hbm_spec():
    return pl.BlockSpec(memory_space=pl.ANY)


def whole_spec(shape):
    return pl.BlockSpec(shape, lambda *_: (0,) * len(shape))


def wall_rows(flip, rows, devices, tables, fields, wall_operator):
    width = wall_operator.shape[0]
    planes = fields.shape[0]
    depth = 2 * planes
    units = 2 * rows // devices
    strip = 3 * depth

    def body(me_ref, offset_ref, count_ref, fields_ref, wall_ref, *refs):
        outs, held = refs[:-1], refs[-1]
        me, group = me_ref[0], me_ref[1]
        middle, end = sent_runs(count_ref, group, flip)
        begins = offset_ref[group, group ^ flip], offset_ref[group, group ^ flip ^ 1] - middle

        def source(i):
            return jnp.where(i < end, i + jnp.where(i < middle, begins[0], begins[1]), 0)

        for s in range(0, devices, 2):
            for u in range(units):
                row = source(u * (devices // 2) + lax.shift_right_logical(me ^ s, 1))
                column = pl.multiple_of(row * width, width)
                for field in range(3):
                    at = u * strip + field * depth
                    held[at : at + depth] = fields_ref[:, field, :, pl.ds(column, width)].reshape(depth, width)
            walled = jnp.dot(held[...], wall_ref[...], preferred_element_type=F32).astype(BF16)
            halves = walled[:, :LANES], walled[:, LANES:]
            swapped = (me & 1) == 1
            for t in range(2):
                block = jnp.where(swapped, halves[1 - t], halves[t])
                for u in range(units):
                    for field in range(3):
                        at = u * strip + field * depth
                        outs[s + t][u, field] = block[at : at + depth]

    shape = (units, 3, depth, LANES)
    return pl.pallas_call(
        body,
        grid_spec=pltpu.PrefetchScalarGridSpec(
            num_scalar_prefetch=3,
            grid=(1,),
            in_specs=[whole_spec(fields.shape), whole_spec(wall_operator.shape)],
            out_specs=[whole_spec(shape)] * devices,
            scratch_shapes=[pltpu.VMEM((units * strip, width), BF16)],
        ),
        out_shape=[jax.ShapeDtypeStruct(shape, BF16)] * devices,
        compiler_params=PARAMS,
        cost_estimate=pl.CostEstimate(
            flops=rows * 12 * planes * width * width, bytes_accessed=12 * planes * width * (rows + 32), transcendentals=0
        ),
    )(*tables, fields, wall_operator)


def transform(me, pencil, matrix, factors):
    devices = len(pencil)
    units, _, depth, lanes = pencil[0].shape
    size = devices * depth
    strip = 3 * lanes

    def body(me_ref, *refs):
        ins, (matrix_ref, factors_ref) = refs[:devices], refs[devices : devices + 2]
        outs, (block, turned, scale) = refs[devices + 2 : -3], refs[-3:]
        for s in range(devices):
            at = pl.ds(pl.multiple_of((me_ref[0] ^ s) * depth, depth), depth)
            turned[s * depth : (s + 1) * depth] = matrix_ref[at]
            for k in range(2):
                scale[k, s * depth : (s + 1) * depth] = factors_ref[k, at]
            for u in range(units):
                for f in range(3):
                    column = u * strip + f * lanes
                    block[at, column : column + lanes] = ins[s][u, f]
        for u in range(units):
            modes = jnp.dot(turned[...], block[:, u * strip : (u + 1) * strip], preferred_element_type=F32)
            velocity, buoyant, magnetic = (modes[:, f * lanes : f * lanes + lanes] for f in range(3))
            damping, wave = scale[0], scale[1]
            coupled = (
                damping * (velocity + STEP_DT * buoyant + wave * magnetic),
                damping * (buoyant - STEP_DT * velocity),
                damping * (magnetic - wave * velocity),
            )
            for f in range(3):
                rounded = coupled[f].astype(BF16)
                for s in range(devices):
                    outs[s][u, f] = rounded[s * depth : (s + 1) * depth]

    spec = whole_spec(pencil[0].shape)
    return pl.pallas_call(
        body,
        grid_spec=pltpu.PrefetchScalarGridSpec(
            num_scalar_prefetch=1,
            grid=(1,),
            in_specs=[spec] * devices + [whole_spec(matrix.shape), whole_spec(factors.shape)],
            out_specs=[spec] * devices,
            scratch_shapes=[
                pltpu.VMEM((size, units * strip), BF16),
                pltpu.VMEM((size, size), BF16),
                pltpu.VMEM((2, size, lanes), F32),
            ],
        ),
        out_shape=[jax.ShapeDtypeStruct(pencil[0].shape, BF16)] * devices,
        compiler_params=PARAMS,
        cost_estimate=pl.CostEstimate(
            flops=units * 6 * size * size * lanes, bytes_accessed=units * 12 * size * lanes, transcendentals=0
        ),
    )(me, *pencil, matrix, factors)


def bring(buffers, held, sem):
    copies, first = [], 0
    for b, buffer in enumerate(buffers):
        size = buffer.shape[0]
        copies.append(pltpu.make_async_copy(buffer, held.at[pl.ds(first, size)], sem.at[b]))
        first += size
    for copy in copies:
        copy.start()
    return copies


def windows(me, count, pieces, wanted):
    buffers = [b for _, piece in pieces for b in piece]
    sizes = [sum(b.shape[0] for b in piece) for _, piece in pieces]
    bases = {flip: sum(sizes[:p]) for p, (flip, _) in enumerate(pieces)}
    units = {flip: piece[0].shape[0] for flip, piece in pieces}
    devices = len(pieces[0][1])
    unit_shape = buffers[0].shape[1:]
    shape = (2 * SLOT,) + unit_shape

    def body(me_ref, count_ref, *refs):
        ins, outs, (held, sem) = refs[: len(buffers)], refs[len(buffers) : -2], refs[-2:]
        copies = bring(ins, held, sem)
        group = me_ref[1]
        starts = {(flip, 0): 0 for flip, _ in pieces}
        starts |= {(flip, 1): 2 * sent_runs(count_ref, group ^ flip, flip)[0] for flip, _ in pieces}
        for copy in copies:
            copy.wait()
        for out, (flip, to) in zip(outs, wanted):
            for slot in range(2 * SLOT):
                unit = jnp.minimum(starts[flip, to] + slot, devices * units[flip] - 1)
                owner = (unit & (devices - 1)) ^ me_ref[0]
                level = lax.shift_right_logical(unit, devices.bit_length() - 1)
                out[slot] = held[bases[flip] + owner * units[flip] + level]

    return pl.pallas_call(
        body,
        grid_spec=pltpu.PrefetchScalarGridSpec(
            num_scalar_prefetch=2,
            grid=(1,),
            in_specs=[hbm_spec()] * len(buffers),
            out_specs=[whole_spec(shape)] * len(wanted),
            scratch_shapes=[pltpu.VMEM((sum(sizes),) + unit_shape, BF16), pltpu.SemaphoreType.DMA((len(buffers),))],
        ),
        out_shape=[jax.ShapeDtypeStruct(shape, BF16)] * len(wanted),
        compiler_params=PARAMS,
        cost_estimate=pl.CostEstimate(flops=0, bytes_accessed=2**21 * len(wanted), transcendentals=0),
    )(me, count, *buffers)


def place_rows(me, count, held, rows_dev, width):
    _, _, depth, lanes = held[0].shape
    planes, step = depth // 2, 8

    def body(me_ref, count_ref, *refs):
        ins, out_ref, (held, units, sem) = refs[:-4], refs[-4], refs[-3:]
        group = me_ref[1]
        blank = 2 * SLOT * len(SENDERS)

        now = pl.program_id(0)

        def copies(i):
            planes_of = pl.ds(pl.multiple_of(i * 2 * step, 2 * step), 2 * step)
            return [
                pltpu.make_async_copy(
                    ref.at[:, :, planes_of], held.at[pl.ds(2 * SLOT * w, 2 * SLOT), :, planes_of], sem.at[i, w]
                )
                for w, ref in enumerate(ins)
            ]

        @pl.when(now == 0)
        def _():
            for i in range(planes // step):
                for copy in copies(i):
                    copy.start()
            held[blank : blank + 2] = jnp.zeros((2,) + held.shape[1:], BF16)

            ends = [0]
            for sender in range(len(SENDERS)):
                ends.append(ends[-1] + count_ref[sender, group])
            for row in range(rows_dev):
                sender, slot = 0, row
                for g in range(1, len(SENDERS)):
                    later = row >= ends[g]
                    sender = jnp.where(later, g, sender)
                    slot = jnp.where(later, row - ends[g], slot)
                window = 0
                for j, flip in enumerate(SENDERS):
                    window = jnp.where((sender ^ group) == flip, j, window)
                units[row] = jnp.where(row < ends[-1], 2 * (SLOT * window + slot), blank)

        for copy in copies(now):
            copy.wait()
        here = pl.ds(pl.multiple_of(now * 2 * step, 2 * step), 2 * step)
        for row in range(rows_dev):
            for half in range(2):
                at = units[row] + half
                column = row * width + half * lanes
                for field in range(3):
                    block = held[at, field, here].astype(F32).reshape(step, 2, lanes)
                    out_ref[:, field, :, column : column + lanes] = block

    return pl.pallas_call(
        body,
        grid_spec=pltpu.PrefetchScalarGridSpec(
            num_scalar_prefetch=2,
            grid=(planes // step,),
            in_specs=[hbm_spec()] * len(held),
            out_specs=pl.BlockSpec((step, 3, 2, rows_dev * width), lambda i, *_: (i, 0, 0, 0)),
            scratch_shapes=[
                pltpu.VMEM((2 * SLOT * len(SENDERS) + 2, 3, depth, lanes), BF16),
                pltpu.SMEM((rows_dev,), jnp.int32),
                pltpu.SemaphoreType.DMA((planes // step, len(held))),
            ],
        ),
        out_shape=jax.ShapeDtypeStruct((planes, 3, 2, rows_dev * width), F32),
        compiler_params=PARAMS,
        cost_estimate=pl.CostEstimate(
            flops=0, bytes_accessed=rows_dev * 36 * planes * width, transcendentals=0
        ),
    )(me, count, *held)


def after(values, earlier):
    return list(lax.optimization_barrier((tuple(values), earlier))[0])


def permute(value, s, flip):
    devices, groups = lax.axis_size("gz"), lax.axis_size("ky")
    pairs = [(d * groups + g, (d ^ s) * groups + (g ^ flip)) for d in range(devices) for g in range(groups)]
    return lax.ppermute(value, ("gz", "ky"), pairs)


def exchange(buffers, flip):
    out = list(buffers)
    for s in reversed(range(0 if flip else 1, len(buffers))):
        out[s] = permute(buffers[s], s, flip)
    return out


def run(sizes, tables, fields, wall_operator, matrix, factors):
    devices = lax.axis_size("gz")
    me, _, count = tables
    pencils = []
    for flip, rows in zip(FLIPS, sizes):
        walled = wall_rows(flip, rows, devices, tables, fields, wall_operator)
        if sizes[0] < sizes[1]:
            tables = (after([me], walled[1])[0],) + tables[1:]
        pencils.append(exchange(walled, flip))
    first, second = (list(transform(me, pencil, matrix, factors)) for pencil in pencils)
    pieces = [(FLIPS[0], exchange(first, 0)), (FLIPS[1], exchange(second, 0))]
    if sizes[0] < sizes[1]:
        far, far_sent = windows(me, count, pieces[:1], [(2, 0), (2, 1)])
        near, near_sent = windows(me, count, pieces[1:], [(0, 0), (0, 1)])
    else:
        near_sent, far_sent = windows(me, count, pieces, [(0, 1), (2, 1)])
        near, far = windows(me, count, pieces, [(0, 0), (2, 0)])
    return near, far, permute(near_sent, 0, 1), permute(far_sent, 0, 1)


def per_device(fields, wall_operator, remap_offset, remap_count):
    devices = lax.axis_size("gz")
    half_z = fields.shape[0] * devices // 2
    matrix = jnp.asarray(mode_matrix(half_z))
    factors = jnp.asarray(mode_factors(half_z))
    width = wall_operator.shape[0]
    rows_dev = fields.shape[3] // width
    me = jnp.stack([lax.axis_index("gz"), lax.axis_index("ky")]).astype(jnp.int32)
    tables = (me, remap_offset, remap_count)
    sizes = [size for size in (12, 16) if 2 * size % devices == 0]
    branches = [functools.partial(run, (far, near)) for far in sizes for near in sizes]
    arguments = (tables, fields, wall_operator, matrix, factors)
    if len(branches) == 1:
        held = branches[0](*arguments)
    else:
        held = lax.switch(choose(remap_count, sizes), branches, *arguments)
    return place_rows(me, remap_count, held, rows_dev, width)


def solution(mesh):
    placed = (P("gz", None, None, "ky"), P(), P(), P())
    return jax.shard_map(
        per_device, mesh=mesh, in_specs=placed, out_specs=P("gz", None, None, "ky"), check_vma=False
    )
```

profile of v0, /device:TPU:17, one launch (start us, length us, event | category | flops | bytes accessed | tf_op | source)
XLA Modules:
  0.0 168.4 jit_solution(7841196935055799565)
XLA Ops:
  2.0 159.9 %conditional.1 = (bf16[16,3,64,128]{3,2,1,0:T(8,128)(2,1)S(1)}, bf16[16,3,64,128]{3,2,1,0:T(8,128)(2,1)S(1)}, bf16[16,3,64,128]{3,2,1,0:T(8,128)(2,1)}, bf16[16,3,64,128]{3,2,1,0:T(8,128)(2,1)}) conditional(s32[]{:T(128)} %bitcast.2, (s32[2]{0:T(128)S(1)}, s32[4,4]{1,0:T(4,128)}, s32[4,4]{1,0:T(4,128)}, ...), branch_computations={%region_0.0_spmd, %region_1.0_spmd, %region_2.0_spmd, %region_3.0_... | conditional | flops 2415919104 | bytes 80218488 | solution.py:355
  2.5 4.9 %branch_3_fun.8 = (bf16[4,3,64,128]{3,2,1,0:T(8,128)(2,1)}, bf16[4,3,64,128]{3,2,1,0:T(8,128)(2,1)}, bf16[4,3,64,128]{3,2,1,0:T(8,128)(2,1)}, bf16[4,3,64,128]{3...) custom-call(s32[2]{0:T(128)S(1)} %get-tuple-element.191.me_ref, ...), custom_call_target="tpu_custom_call" | custom-call | flops 402653184 | bytes 4718592 | tf_op jit(solution)/shard_map/cond/branch_3_fun/pallas_call | solution.py:109
  8.7 1.3 collective-permute-start.109
  10.1 3.3 %collective-permute-start.112 = (bf16[4,3,64,128]{3,2,1,0:T(8,128)(2,1)}, bf16[4,3,64,128]{3,2,1,0:T(8,128)(2,1)S(1)}, u32[]{:S(2)}, u32[]{:S(2)}) collective-permute-start(bf16[4,3,64,128]{3,2,1,0:T(8,128)(2,1)} %get-tuple-element.219), channel_id=1, source_target_pairs={{0,20},{1,21},{2,22},{3,23},{4,16},{5,17},{6,18},{7,19},{8,28},{9,... | collective-permute-start | bytes 589832 | tf_op jit(solution)/shard_map/cond/branch_3_fun/ppermute | solution.py:310
  13.4 4.8 %branch_3_fun.6 = (bf16[4,3,64,128]{3,2,1,0:T(8,128)(2,1)}, bf16[4,3,64,128]{3,2,1,0:T(8,128)(2,1)}, bf16[4,3,64,128]{3,2,1,0:T(8,128)(2,1)}, bf16[4,3,64,128]{3...) custom-call(s32[2]{0:T(128)S(1)} %get-tuple-element.191.me_ref, ...), custom_call_target="tpu_custom_call" | custom-call | flops 402653184 | bytes 4718592 | tf_op jit(solution)/shard_map/cond/branch_3_fun/pallas_call | solution.py:109
  19.7 4.0 %collective-permute-done.110.refs_3_ = bf16[4,3,64,128]{3,2,1,0:T(8,128)(2,1)S(1)} collective-permute-done((bf16[4,3,64,128]{3,2,1,0:T(8,128)(2,1)}, bf16[4,3,64,128]{3,2,1,0:T(8,128)(2,1)S(1)}, u32[]{:S(2)}, u32[]{:S(2)}) %collective-permute-start.110) | collective-permute-done | bytes 196640 | tf_op jit(solution)/shard_map/cond/branch_3_fun/ppermute | solution.py:310
  24.9 1.9 %collective-permute-done.112.refs_5_ = bf16[4,3,64,128]{3,2,1,0:T(8,128)(2,1)S(1)} collective-permute-done((bf16[4,3,64,128]{3,2,1,0:T(8,128)(2,1)}, bf16[4,3,64,128]{3,2,1,0:T(8,128)(2,1)S(1)}, u32[]{:S(2)}, u32[]{:S(2)}) %collective-permute-start.112) | collective-permute-done | bytes 196640 | tf_op jit(solution)/shard_map/cond/branch_3_fun/ppermute | solution.py:310
  26.9 13.7 %collective-permute-start.95 = (bf16[4,3,64,128]{3,2,1,0:T(8,128)(2,1)}, bf16[4,3,64,128]{3,2,1,0:T(8,128)(2,1)S(1)}, u32[]{:S(2)}, u32[]{:S(2)}) collective-permute-start(bf16[4,3,64,128]{3,2,1,0:T(8,128)(2,1)} %get-tuple-element.198), channel_id=1, source_target_pairs={{0,10},{1,11},{2,8},{3,9},{4,14},{5,15},{6,12},{7,13},{8,2},{9,3},... | collective-permute-start | bytes 589832 | tf_op jit(solution)/shard_map/cond/branch_3_fun/ppermute | solution.py:310
  41.6 5.3 %collective-permute-done.114.refs_7_ = bf16[4,3,64,128]{3,2,1,0:T(8,128)(2,1)S(1)} collective-permute-done((bf16[4,3,64,128]{3,2,1,0:T(8,128)(2,1)}, bf16[4,3,64,128]{3,2,1,0:T(8,128)(2,1)S(1)}, u32[]{:S(2)}, u32[]{:S(2)}) %collective-permute-start.114) | collective-permute-done | bytes 196640 | tf_op jit(solution)/shard_map/cond/branch_3_fun/ppermute | solution.py:310
  46.9 3.1 %collective-permute-start.98 = (bf16[4,3,64,128]{3,2,1,0:T(8,128)(2,1)}, bf16[4,3,64,128]{3,2,1,0:T(8,128)(2,1)S(1)}, u32[]{:S(2)}, u32[]{:S(2)}) collective-permute-start(bf16[4,3,64,128]{3,2,1,0:T(8,128)(2,1)} %get-tuple-element.201), channel_id=1, source_target_pairs={{0,22},{1,23},{2,20},{3,21},{4,18},{5,19},{6,16},{7,17},{8,30},{9,... | collective-permute-start | bytes 589832 | tf_op jit(solution)/shard_map/cond/branch_3_fun/ppermute | solution.py:310
  50.0 4.1 %collective-permute-start.99 = (bf16[4,3,64,128]{3,2,1,0:T(8,128)(2,1)}, bf16[4,3,64,128]{3,2,1,0:T(8,128)(2,1)S(1)}, u32[]{:S(2)}, u32[]{:S(2)}) collective-permute-start(bf16[4,3,64,128]{3,2,1,0:T(8,128)(2,1)} %get-tuple-element.202), channel_id=1, source_target_pairs={{0,26},{1,27},{2,24},{3,25},{4,30},{5,31},{6,28},{7,29},{8,18},{9,... | collective-permute-start | bytes 589832 | tf_op jit(solution)/shard_map/cond/branch_3_fun/ppermute | solution.py:310
  54.1 4.7 %branch_3_fun.9 = (bf16[4,3,64,128]{3,2,1,0:T(8,128)(2,1)}, bf16[4,3,64,128]{3,2,1,0:T(8,128)(2,1)}, bf16[4,3,64,128]{3,2,1,0:T(8,128)(2,1)}, bf16[4,3,64,128]{3...) custom-call(s32[2]{0:T(128)S(1)} %get-tuple-element.191.me_ref, ...), custom_call_target="tpu_custom_call" | custom-call | flops 805306368 | bytes 3145728 | tf_op jit(solution)/shard_map/cond/branch_3_fun/pallas_call | solution.py:159
  58.8 1.3 collective-permute-start.115
  60.1 2.1 %collective-permute-start.116 = (bf16[4,3,64,128]{3,2,1,0:T(8,128)(2,1)}, bf16[4,3,64,128]{3,2,1,0:T(8,128)(2,1)S(1)}, u32[]{:S(2)}, u32[]{:S(2)}) collective-permute-start(bf16[4,3,64,128]{3,2,1,0:T(8,128)(2,1)} %get-tuple-element.224), channel_id=1, source_target_pairs={{0,8},{1,9},{2,10},{3,11},{4,12},{5,13},{6,14},{7,15},{8,0},{9,1},... | collective-permute-start | bytes 589832 | tf_op jit(solution)/shard_map/cond/branch_3_fun/ppermute | solution.py:310
  62.2 9.1 %collective-permute-done.98.refs_5_ = bf16[4,3,64,128]{3,2,1,0:T(8,128)(2,1)S(1)} collective-permute-done((bf16[4,3,64,128]{3,2,1,0:T(8,128)(2,1)}, bf16[4,3,64,128]{3,2,1,0:T(8,128)(2,1)S(1)}, u32[]{:S(2)}, u32[]{:S(2)}) %collective-permute-start.98) | collective-permute-done | bytes 196640 | tf_op jit(solution)/shard_map/cond/branch_3_fun/ppermute | solution.py:310
  71.3 4.8 %collective-permute-start.117 = (bf16[4,3,64,128]{3,2,1,0:T(8,128)(2,1)}, bf16[4,3,64,128]{3,2,1,0:T(8,128)(2,1)S(1)}, u32[]{:S(2)}, u32[]{:S(2)}) collective-permute-start(bf16[4,3,64,128]{3,2,1,0:T(8,128)(2,1)} %get-tuple-element.225), channel_id=1, source_target_pairs={{0,12},{1,13},{2,14},{3,15},{4,8},{5,9},{6,10},{7,11},{8,4},{9,5},... | collective-permute-start | bytes 589832 | tf_op jit(solution)/shard_map/cond/branch_3_fun/ppermute | solution.py:310
  76.1 2.1 %collective-permute-done.99.refs_6_ = bf16[4,3,64,128]{3,2,1,0:T(8,128)(2,1)S(1)} collective-permute-done((bf16[4,3,64,128]{3,2,1,0:T(8,128)(2,1)}, bf16[4,3,64,128]{3,2,1,0:T(8,128)(2,1)S(1)}, u32[]{:S(2)}, u32[]{:S(2)}) %collective-permute-start.99) | collective-permute-done | bytes 196640 | tf_op jit(solution)/shard_map/cond/branch_3_fun/ppermute | solution.py:310
  78.2 7.6 %collective-permute-done.100.refs_7_ = bf16[4,3,64,128]{3,2,1,0:T(8,128)(2,1)S(1)} collective-permute-done((bf16[4,3,64,128]{3,2,1,0:T(8,128)(2,1)}, bf16[4,3,64,128]{3,2,1,0:T(8,128)(2,1)S(1)}, u32[]{:S(2)}, u32[]{:S(2)}) %collective-permute-start.100) | collective-permute-done | bytes 196640 | tf_op jit(solution)/shard_map/cond/branch_3_fun/ppermute | solution.py:310
  86.5 4.6 %branch_3_fun.7 = (bf16[4,3,64,128]{3,2,1,0:T(8,128)(2,1)}, bf16[4,3,64,128]{3,2,1,0:T(8,128)(2,1)}, bf16[4,3,64,128]{3,2,1,0:T(8,128)(2,1)}, bf16[4,3,64,128]{3...) custom-call(s32[2]{0:T(128)S(1)} %get-tuple-element.191.me_ref, ...), custom_call_target="tpu_custom_call" | custom-call | flops 805306368 | bytes 3145728 | tf_op jit(solution)/shard_map/cond/branch_3_fun/pallas_call | solution.py:159
  91.3 2.5 %collective-permute-start.101 = (bf16[4,3,64,128]{3,2,1,0:T(8,128)(2,1)}, bf16[4,3,64,128]{3,2,1,0:T(8,128)(2,1)S(1)}, u32[]{:S(2)}, u32[]{:S(2)}) collective-permute-start(bf16[4,3,64,128]{3,2,1,0:T(8,128)(2,1)} %get-tuple-element.207), channel_id=1, source_target_pairs={{0,4},{1,5},{2,6},{3,7},{4,0},{5,1},{6,2},{7,3},{8,12},{9,13},{10,... | collective-permute-start | bytes 589832 | tf_op jit(solution)/shard_map/cond/branch_3_fun/ppermute | solution.py:310
  93.8 2.1 %collective-permute-start.102 = (bf16[4,3,64,128]{3,2,1,0:T(8,128)(2,1)}, bf16[4,3,64,128]{3,2,1,0:T(8,128)(2,1)S(1)}, u32[]{:S(2)}, u32[]{:S(2)}) collective-permute-start(bf16[4,3,64,128]{3,2,1,0:T(8,128)(2,1)} %get-tuple-element.208), channel_id=1, source_target_pairs={{0,8},{1,9},{2,10},{3,11},{4,12},{5,13},{6,14},{7,15},{8,0},{9,1},... | collective-permute-start | bytes 589832 | tf_op jit(solution)/shard_map/cond/branch_3_fun/ppermute | solution.py:310
  96.6 9.0 %collective-permute-start.103 = (bf16[4,3,64,128]{3,2,1,0:T(8,128)(2,1)}, bf16[4,3,64,128]{3,2,1,0:T(8,128)(2,1)S(1)}, u32[]{:S(2)}, u32[]{:S(2)}) collective-permute-start(bf16[4,3,64,128]{3,2,1,0:T(8,128)(2,1)} %get-tuple-element.209), channel_id=1, source_target_pairs={{0,12},{1,13},{2,14},{3,15},{4,8},{5,9},{6,10},{7,11},{8,4},{9,5},... | collective-permute-start | bytes 589832 | tf_op jit(solution)/shard_map/cond/branch_3_fun/ppermute | solution.py:310
  105.6 6.3 %collective-permute-done.120.refs_14_ = bf16[4,3,64,128]{3,2,1,0:T(8,128)(2,1)S(1)} collective-permute-done((bf16[4,3,64,128]{3,2,1,0:T(8,128)(2,1)}, bf16[4,3,64,128]{3,2,1,0:T(8,128)(2,1)S(1)}, u32[]{:S(2)}, u32[]{:S(2)}) %collective-permute-start.120) | collective-permute-done | bytes 196640 | tf_op jit(solution)/shard_map/cond/branch_3_fun/ppermute | solution.py:310
  112.0 8.7 %collective-permute-done.121.refs_15_ = bf16[4,3,64,128]{3,2,1,0:T(8,128)(2,1)S(1)} collective-permute-done((bf16[4,3,64,128]{3,2,1,0:T(8,128)(2,1)}, bf16[4,3,64,128]{3,2,1,0:T(8,128)(2,1)S(1)}, u32[]{:S(2)}, u32[]{:S(2)}) %collective-permute-start.121) | collective-permute-done | bytes 196640 | tf_op jit(solution)/shard_map/cond/branch_3_fun/ppermute | solution.py:310
  120.9 7.3 %collective-permute-done.104.refs_4_ = bf16[4,3,64,128]{3,2,1,0:T(8,128)(2,1)S(1)} collective-permute-done((bf16[4,3,64,128]{3,2,1,0:T(8,128)(2,1)}, bf16[4,3,64,128]{3,2,1,0:T(8,128)(2,1)S(1)}, u32[]{:S(2)}, u32[]{:S(2)}) %collective-permute-start.104) | collective-permute-done | bytes 196640 | tf_op jit(solution)/shard_map/cond/branch_3_fun/ppermute | solution.py:310
  128.2 4.3 %collective-permute-done.105.refs_5_ = bf16[4,3,64,128]{3,2,1,0:T(8,128)(2,1)S(1)} collective-permute-done((bf16[4,3,64,128]{3,2,1,0:T(8,128)(2,1)}, bf16[4,3,64,128]{3,2,1,0:T(8,128)(2,1)S(1)}, u32[]{:S(2)}, u32[]{:S(2)}) %collective-permute-start.105) | collective-permute-done | bytes 196640 | tf_op jit(solution)/shard_map/cond/branch_3_fun/ppermute | solution.py:310
  132.5 13.2 %collective-permute-done.106.refs_6_ = bf16[4,3,64,128]{3,2,1,0:T(8,128)(2,1)S(1)} collective-permute-done((bf16[4,3,64,128]{3,2,1,0:T(8,128)(2,1)}, bf16[4,3,64,128]{3,2,1,0:T(8,128)(2,1)S(1)}, u32[]{:S(2)}, u32[]{:S(2)}) %collective-permute-start.106) | collective-permute-done | bytes 196640 | tf_op jit(solution)/shard_map/cond/branch_3_fun/ppermute | solution.py:310
  145.7 6.6 %collective-permute-done.107.refs_7_ = bf16[4,3,64,128]{3,2,1,0:T(8,128)(2,1)S(1)} collective-permute-done((bf16[4,3,64,128]{3,2,1,0:T(8,128)(2,1)}, bf16[4,3,64,128]{3,2,1,0:T(8,128)(2,1)S(1)}, u32[]{:S(2)}, u32[]{:S(2)}) %collective-permute-start.107) | collective-permute-done | bytes 196640 | tf_op jit(solution)/shard_map/cond/branch_3_fun/ppermute | solution.py:310
  152.9 3.9 %branch_3_fun.11 = (bf16[16,3,64,128]{3,2,1,0:T(8,128)(2,1)}, bf16[16,3,64,128]{3,2,1,0:T(8,128)(2,1)}) custom-call(s32[2]{0:T(128)S(1)} %get-tuple-element.191.me_ref, s32[4,4]{1,0:T(4,128)S(1)} %copy-done.24, bf16[4,3,64,128]{3,2,1,0:T(8,128)(2,1)} %get-tuple-element.206.refs_0_, bf16[4,3,64,128]{3,2,1,0:T(8,128)(2,1)} %copy-done.7, ...), custom_call_target="tpu_custom_call" | custom-call | bytes 4194304 | tf_op jit(solution)/shard_map/cond/branch_3_fun/pallas_call | solution.py:215
  156.8 1.7 collective-permute-start.122
  158.5 2.7 %branch_3_fun.10 = (bf16[16,3,64,128]{3,2,1,0:T(8,128)(2,1)S(1)}, bf16[16,3,64,128]{3,2,1,0:T(8,128)(2,1)S(1)}) custom-call(s32[2]{0:T(128)S(1)} %get-tuple-element.191.me_ref, s32[4,4]{1,0:T(4,128)S(1)} %copy-done.24, bf16[4,3,64,128]{3,2,1,0:T(8,128)(2,1)} %get-tuple-element.206.refs_0_, bf16[4,3,64,128]{3,2,1,0:T(8,128)(2,1)} %copy-done.7, ...), custom_call_target="tpu_custom_call" | custom-call | bytes 4194304 | tf_op jit(solution)/shard_map/cond/branch_3_fun/pallas_call | solution.py:215
  161.8 6.3 %shard_map.65 = f32[32,3,2,8192]{3,2,1,0:T(2,128)} custom-call(s32[2]{0:T(128)S(1)} %pad_add_fusion.me_ref, s32[4,4]{1,0:T(4,128)} %count_ref.3, bf16[16,3,64,128]{3,2,1,0:T(8,128)(2,1)S(1)} %get-tuple-element.238.refs_0_, bf16[16,3,64,128]{3,2,1,0:T(8,128)(2,1)S(1)} %get-tuple-element.239.refs_1_, bf16[16,3,64,128]{3,2,1,0:T(8,128)(2,1)} %get-tuple-element.240.refs_2_, ...), custom_call_target="tpu_custom_call" | custom-call | bytes 9437184 | tf_op jit(solution)/shard_map/pallas_call | solution.py:282
  (104 shorter events, 9.3 us)
Async XLA Ops:
  2.5 150.4 %copy-start.24 = (s32[4,4]{1,0:T(4,128)S(1)}, s32[4,4]{1,0:T(4,128)}, u32[]{:S(2)}) copy-start(s32[4,4]{1,0:T(4,128)} %get-tuple-element.192.count_ref) | copy-start | bytes 196 | tf_op jit(solution)/shard_map/cond
  7.4 10.8 %collective-permute-start.108 = (bf16[4,3,64,128]{3,2,1,0:T(8,128)(2,1)}, bf16[4,3,64,128]{3,2,1,0:T(8,128)(2,1)S(1)}, u32[]{:S(2)}, u32[]{:S(2)}) collective-permute-start(bf16[4,3,64,128]{3,2,1,0:T(8,128)(2,1)} %get-tuple-element.215), channel_id=1, source_target_pairs={{0,4},{1,5},{2,6},{3,7},{4,0},{5,1},{6,2},{7,3},{8,12},{9,13},{10,... | collective-permute-start | bytes 589832 | tf_op jit(solution)/shard_map/cond/branch_3_fun/ppermute | solution.py:310
  8.7 9.8 %collective-permute-start.109 = (bf16[4,3,64,128]{3,2,1,0:T(8,128)(2,1)}, bf16[4,3,64,128]{3,2,1,0:T(8,128)(2,1)S(1)}, u32[]{:S(2)}, u32[]{:S(2)}) collective-permute-start(bf16[4,3,64,128]{3,2,1,0:T(8,128)(2,1)} %get-tuple-element.216), channel_id=1, source_target_pairs={{0,8},{1,9},{2,10},{3,11},{4,12},{5,13},{6,14},{7,15},{8,0},{9,1},... | collective-permute-start | bytes 589832 | tf_op jit(solution)/shard_map/cond/branch_3_fun/ppermute | solution.py:310
  10.0 13.7 %collective-permute-start.110 = (bf16[4,3,64,128]{3,2,1,0:T(8,128)(2,1)}, bf16[4,3,64,128]{3,2,1,0:T(8,128)(2,1)S(1)}, u32[]{:S(2)}, u32[]{:S(2)}) collective-permute-start(bf16[4,3,64,128]{3,2,1,0:T(8,128)(2,1)} %get-tuple-element.217), channel_id=1, source_target_pairs={{0,12},{1,13},{2,14},{3,15},{4,8},{5,9},{6,10},{7,11},{8,4},{9,5},... | collective-permute-start | bytes 589832 | tf_op jit(solution)/shard_map/cond/branch_3_fun/ppermute | solution.py:310
  10.1 14.9 %collective-permute-start.111 = (bf16[4,3,64,128]{3,2,1,0:T(8,128)(2,1)}, bf16[4,3,64,128]{3,2,1,0:T(8,128)(2,1)S(1)}, u32[]{:S(2)}, u32[]{:S(2)}) collective-permute-start(bf16[4,3,64,128]{3,2,1,0:T(8,128)(2,1)} %get-tuple-element.218), channel_id=1, source_target_pairs={{0,16},{1,17},{2,18},{3,19},{4,20},{5,21},{6,22},{7,23},{8,24},{9,... | collective-permute-start | bytes 589832 | tf_op jit(solution)/shard_map/cond/branch_3_fun/ppermute | solution.py:310
  10.1 16.8 %collective-permute-start.112 = (bf16[4,3,64,128]{3,2,1,0:T(8,128)(2,1)}, bf16[4,3,64,128]{3,2,1,0:T(8,128)(2,1)S(1)}, u32[]{:S(2)}, u32[]{:S(2)}) collective-permute-start(bf16[4,3,64,128]{3,2,1,0:T(8,128)(2,1)} %get-tuple-element.219), channel_id=1, source_target_pairs={{0,20},{1,21},{2,22},{3,23},{4,16},{5,17},{6,18},{7,19},{8,28},{9,... | collective-permute-start | bytes 589832 | tf_op jit(solution)/shard_map/cond/branch_3_fun/ppermute | solution.py:310
  18.2 23.4 %collective-permute-start.113 = (bf16[4,3,64,128]{3,2,1,0:T(8,128)(2,1)}, bf16[4,3,64,128]{3,2,1,0:T(8,128)(2,1)S(1)}, u32[]{:S(2)}, u32[]{:S(2)}) collective-permute-start(bf16[4,3,64,128]{3,2,1,0:T(8,128)(2,1)} %get-tuple-element.220), channel_id=1, source_target_pairs={{0,24},{1,25},{2,26},{3,27},{4,28},{5,29},{6,30},{7,31},{8,16},{9,... | collective-permute-start | bytes 589832 | tf_op jit(solution)/shard_map/cond/branch_3_fun/ppermute | solution.py:310
  18.5 28.4 %collective-permute-start.114 = (bf16[4,3,64,128]{3,2,1,0:T(8,128)(2,1)}, bf16[4,3,64,128]{3,2,1,0:T(8,128)(2,1)S(1)}, u32[]{:S(2)}, u32[]{:S(2)}) collective-permute-start(bf16[4,3,64,128]{3,2,1,0:T(8,128)(2,1)} %get-tuple-element.221), channel_id=1, source_target_pairs={{0,28},{1,29},{2,30},{3,31},{4,24},{5,25},{6,26},{7,27},{8,20},{9,... | collective-permute-start | bytes 589832 | tf_op jit(solution)/shard_map/cond/branch_3_fun/ppermute | solution.py:310
  23.7 23.1 %collective-permute-start.93 = (bf16[4,3,64,128]{3,2,1,0:T(8,128)(2,1)}, bf16[4,3,64,128]{3,2,1,0:T(8,128)(2,1)S(1)}, u32[]{:S(2)}, u32[]{:S(2)}) collective-permute-start(bf16[4,3,64,128]{3,2,1,0:T(8,128)(2,1)} %get-tuple-element.196), channel_id=1, source_target_pairs={{0,2},{1,3},{2,0},{3,1},{4,6},{5,7},{6,4},{7,5},{8,10},{9,11},{10,... | collective-permute-start | bytes 589832 | tf_op jit(solution)/shard_map/cond/branch_3_fun/ppermute | solution.py:310
  24.9 25.0 %collective-permute-start.94 = (bf16[4,3,64,128]{3,2,1,0:T(8,128)(2,1)}, bf16[4,3,64,128]{3,2,1,0:T(8,128)(2,1)S(1)}, u32[]{:S(2)}, u32[]{:S(2)}) collective-permute-start(bf16[4,3,64,128]{3,2,1,0:T(8,128)(2,1)} %get-tuple-element.197), channel_id=1, source_target_pairs={{0,6},{1,7},{2,4},{3,5},{4,2},{5,3},{6,0},{7,1},{8,14},{9,15},{10,... | collective-permute-start | bytes 589832 | tf_op jit(solution)/shard_map/cond/branch_3_fun/ppermute | solution.py:310
  26.9 27.2 %collective-permute-start.95 = (bf16[4,3,64,128]{3,2,1,0:T(8,128)(2,1)}, bf16[4,3,64,128]{3,2,1,0:T(8,128)(2,1)S(1)}, u32[]{:S(2)}, u32[]{:S(2)}) collective-permute-start(bf16[4,3,64,128]{3,2,1,0:T(8,128)(2,1)} %get-tuple-element.198), channel_id=1, source_target_pairs={{0,10},{1,11},{2,8},{3,9},{4,14},{5,15},{6,12},{7,13},{8,2},{9,3},... | collective-permute-start | bytes 589832 | tf_op jit(solution)/shard_map/cond/branch_3_fun/ppermute | solution.py:310
  41.6 17.2 %collective-permute-start.96 = (bf16[4,3,64,128]{3,2,1,0:T(8,128)(2,1)}, bf16[4,3,64,128]{3,2,1,0:T(8,128)(2,1)S(1)}, u32[]{:S(2)}, u32[]{:S(2)}) collective-permute-start(bf16[4,3,64,128]{3,2,1,0:T(8,128)(2,1)} %get-tuple-element.199), channel_id=1, source_target_pairs={{0,14},{1,15},{2,12},{3,13},{4,10},{5,11},{6,8},{7,9},{8,6},{9,7},... | collective-permute-start | bytes 589832 | tf_op jit(solution)/shard_map/cond/branch_3_fun/ppermute | solution.py:310
  46.8 13.3 %collective-permute-start.97 = (bf16[4,3,64,128]{3,2,1,0:T(8,128)(2,1)}, bf16[4,3,64,128]{3,2,1,0:T(8,128)(2,1)S(1)}, u32[]{:S(2)}, u32[]{:S(2)}) collective-permute-start(bf16[4,3,64,128]{3,2,1,0:T(8,128)(2,1)} %get-tuple-element.200), channel_id=1, source_target_pairs={{0,18},{1,19},{2,16},{3,17},{4,22},{5,23},{6,20},{7,21},{8,26},{9,... | collective-permute-start | bytes 589832 | tf_op jit(solution)/shard_map/cond/branch_3_fun/ppermute | solution.py:310
  46.9 24.4 %collective-permute-start.98 = (bf16[4,3,64,128]{3,2,1,0:T(8,128)(2,1)}, bf16[4,3,64,128]{3,2,1,0:T(8,128)(2,1)S(1)}, u32[]{:S(2)}, u32[]{:S(2)}) collective-permute-start(bf16[4,3,64,128]{3,2,1,0:T(8,128)(2,1)} %get-tuple-element.201), channel_id=1, source_target_pairs={{0,22},{1,23},{2,20},{3,21},{4,18},{5,19},{6,16},{7,17},{8,30},{9,... | collective-permute-start | bytes 589832 | tf_op jit(solution)/shard_map/cond/branch_3_fun/ppermute | solution.py:310
  50.0 28.3 %collective-permute-start.99 = (bf16[4,3,64,128]{3,2,1,0:T(8,128)(2,1)}, bf16[4,3,64,128]{3,2,1,0:T(8,128)(2,1)S(1)}, u32[]{:S(2)}, u32[]{:S(2)}) collective-permute-start(bf16[4,3,64,128]{3,2,1,0:T(8,128)(2,1)} %get-tuple-element.202), channel_id=1, source_target_pairs={{0,26},{1,27},{2,24},{3,25},{4,30},{5,31},{6,28},{7,29},{8,18},{9,... | collective-permute-start | bytes 589832 | tf_op jit(solution)/shard_map/cond/branch_3_fun/ppermute | solution.py:310
  54.1 31.7 %collective-permute-start.100 = (bf16[4,3,64,128]{3,2,1,0:T(8,128)(2,1)}, bf16[4,3,64,128]{3,2,1,0:T(8,128)(2,1)S(1)}, u32[]{:S(2)}, u32[]{:S(2)}) collective-permute-start(bf16[4,3,64,128]{3,2,1,0:T(8,128)(2,1)} %get-tuple-element.203), channel_id=1, source_target_pairs={{0,30},{1,31},{2,28},{3,29},{4,26},{5,27},{6,24},{7,25},{8,22},{9,... | collective-permute-start | bytes 589832 | tf_op jit(solution)/shard_map/cond/branch_3_fun/ppermute | solution.py:310
  58.8 32.3 %collective-permute-start.115 = (bf16[4,3,64,128]{3,2,1,0:T(8,128)(2,1)}, bf16[4,3,64,128]{3,2,1,0:T(8,128)(2,1)S(1)}, u32[]{:S(2)}, u32[]{:S(2)}) collective-permute-start(bf16[4,3,64,128]{3,2,1,0:T(8,128)(2,1)} %get-tuple-element.223), channel_id=1, source_target_pairs={{0,4},{1,5},{2,6},{3,7},{4,0},{5,1},{6,2},{7,3},{8,12},{9,13},{10,... | collective-permute-start | bytes 589832 | tf_op jit(solution)/shard_map/cond/branch_3_fun/ppermute | solution.py:310
  60.1 31.1 %collective-permute-start.116 = (bf16[4,3,64,128]{3,2,1,0:T(8,128)(2,1)}, bf16[4,3,64,128]{3,2,1,0:T(8,128)(2,1)S(1)}, u32[]{:S(2)}, u32[]{:S(2)}) collective-permute-start(bf16[4,3,64,128]{3,2,1,0:T(8,128)(2,1)} %get-tuple-element.224), channel_id=1, source_target_pairs={{0,8},{1,9},{2,10},{3,11},{4,12},{5,13},{6,14},{7,15},{8,0},{9,1},... | collective-permute-start | bytes 589832 | tf_op jit(solution)/shard_map/cond/branch_3_fun/ppermute | solution.py:310
  71.3 20.0 %collective-permute-start.117 = (bf16[4,3,64,128]{3,2,1,0:T(8,128)(2,1)}, bf16[4,3,64,128]{3,2,1,0:T(8,128)(2,1)S(1)}, u32[]{:S(2)}, u32[]{:S(2)}) collective-permute-start(bf16[4,3,64,128]{3,2,1,0:T(8,128)(2,1)} %get-tuple-element.225), channel_id=1, source_target_pairs={{0,12},{1,13},{2,14},{3,15},{4,8},{5,9},{6,10},{7,11},{8,4},{9,5},... | collective-permute-start | bytes 589832 | tf_op jit(solution)/shard_map/cond/branch_3_fun/ppermute | solution.py:310
  78.2 15.6 %collective-permute-start.118 = (bf16[4,3,64,128]{3,2,1,0:T(8,128)(2,1)}, bf16[4,3,64,128]{3,2,1,0:T(8,128)(2,1)S(1)}, u32[]{:S(2)}, u32[]{:S(2)}) collective-permute-start(bf16[4,3,64,128]{3,2,1,0:T(8,128)(2,1)} %get-tuple-element.226), channel_id=1, source_target_pairs={{0,16},{1,17},{2,18},{3,19},{4,20},{5,21},{6,22},{7,23},{8,24},{9,... | collective-permute-start | bytes 589832 | tf_op jit(solution)/shard_map/cond/branch_3_fun/ppermute | solution.py:310
  85.8 10.8 %collective-permute-start.119 = (bf16[4,3,64,128]{3,2,1,0:T(8,128)(2,1)}, bf16[4,3,64,128]{3,2,1,0:T(8,128)(2,1)S(1)}, u32[]{:S(2)}, u32[]{:S(2)}) collective-permute-start(bf16[4,3,64,128]{3,2,1,0:T(8,128)(2,1)} %get-tuple-element.227), channel_id=1, source_target_pairs={{0,20},{1,21},{2,22},{3,23},{4,16},{5,17},{6,18},{7,19},{8,28},{9,... | collective-permute-start | bytes 589832 | tf_op jit(solution)/shard_map/cond/branch_3_fun/ppermute | solution.py:310
  91.1 20.9 %collective-permute-start.120 = (bf16[4,3,64,128]{3,2,1,0:T(8,128)(2,1)}, bf16[4,3,64,128]{3,2,1,0:T(8,128)(2,1)S(1)}, u32[]{:S(2)}, u32[]{:S(2)}) collective-permute-start(bf16[4,3,64,128]{3,2,1,0:T(8,128)(2,1)} %get-tuple-element.228), channel_id=1, source_target_pairs={{0,24},{1,25},{2,26},{3,27},{4,28},{5,29},{6,30},{7,31},{8,16},{9,... | collective-permute-start | bytes 589832 | tf_op jit(solution)/shard_map/cond/branch_3_fun/ppermute | solution.py:310
  91.2 29.5 %collective-permute-start.121 = (bf16[4,3,64,128]{3,2,1,0:T(8,128)(2,1)}, bf16[4,3,64,128]{3,2,1,0:T(8,128)(2,1)S(1)}, u32[]{:S(2)}, u32[]{:S(2)}) collective-permute-start(bf16[4,3,64,128]{3,2,1,0:T(8,128)(2,1)} %get-tuple-element.229), channel_id=1, source_target_pairs={{0,28},{1,29},{2,30},{3,31},{4,24},{5,25},{6,26},{7,27},{8,20},{9,... | collective-permute-start | bytes 589832 | tf_op jit(solution)/shard_map/cond/branch_3_fun/ppermute | solution.py:310
  91.3 29.4 %collective-permute-start.101 = (bf16[4,3,64,128]{3,2,1,0:T(8,128)(2,1)}, bf16[4,3,64,128]{3,2,1,0:T(8,128)(2,1)S(1)}, u32[]{:S(2)}, u32[]{:S(2)}) collective-permute-start(bf16[4,3,64,128]{3,2,1,0:T(8,128)(2,1)} %get-tuple-element.207), channel_id=1, source_target_pairs={{0,4},{1,5},{2,6},{3,7},{4,0},{5,1},{6,2},{7,3},{8,12},{9,13},{10,... | collective-permute-start | bytes 589832 | tf_op jit(solution)/shard_map/cond/branch_3_fun/ppermute | solution.py:310
  93.8 26.9 %collective-permute-start.102 = (bf16[4,3,64,128]{3,2,1,0:T(8,128)(2,1)}, bf16[4,3,64,128]{3,2,1,0:T(8,128)(2,1)S(1)}, u32[]{:S(2)}, u32[]{:S(2)}) collective-permute-start(bf16[4,3,64,128]{3,2,1,0:T(8,128)(2,1)} %get-tuple-element.208), channel_id=1, source_target_pairs={{0,8},{1,9},{2,10},{3,11},{4,12},{5,13},{6,14},{7,15},{8,0},{9,1},... | collective-permute-start | bytes 589832 | tf_op jit(solution)/shard_map/cond/branch_3_fun/ppermute | solution.py:310
  96.6 24.3 %collective-permute-start.103 = (bf16[4,3,64,128]{3,2,1,0:T(8,128)(2,1)}, bf16[4,3,64,128]{3,2,1,0:T(8,128)(2,1)S(1)}, u32[]{:S(2)}, u32[]{:S(2)}) collective-permute-start(bf16[4,3,64,128]{3,2,1,0:T(8,128)(2,1)} %get-tuple-element.209), channel_id=1, source_target_pairs={{0,12},{1,13},{2,14},{3,15},{4,8},{5,9},{6,10},{7,11},{8,4},{9,5},... | collective-permute-start | bytes 589832 | tf_op jit(solution)/shard_map/cond/branch_3_fun/ppermute | solution.py:310
  112.0 16.2 %collective-permute-start.104 = (bf16[4,3,64,128]{3,2,1,0:T(8,128)(2,1)}, bf16[4,3,64,128]{3,2,1,0:T(8,128)(2,1)S(1)}, u32[]{:S(2)}, u32[]{:S(2)}) collective-permute-start(bf16[4,3,64,128]{3,2,1,0:T(8,128)(2,1)} %get-tuple-element.210), channel_id=1, source_target_pairs={{0,16},{1,17},{2,18},{3,19},{4,20},{5,21},{6,22},{7,23},{8,24},{9,... | collective-permute-start | bytes 589832 | tf_op jit(solution)/shard_map/cond/branch_3_fun/ppermute | solution.py:310
  120.6 11.8 %collective-permute-start.105 = (bf16[4,3,64,128]{3,2,1,0:T(8,128)(2,1)}, bf16[4,3,64,128]{3,2,1,0:T(8,128)(2,1)S(1)}, u32[]{:S(2)}, u32[]{:S(2)}) collective-permute-start(bf16[4,3,64,128]{3,2,1,0:T(8,128)(2,1)} %get-tuple-element.211), channel_id=1, source_target_pairs={{0,20},{1,21},{2,22},{3,23},{4,16},{5,17},{6,18},{7,19},{8,28},{9,... | collective-permute-start | bytes 589832 | tf_op jit(solution)/shard_map/cond/branch_3_fun/ppermute | solution.py:310
  120.7 25.0 %collective-permute-start.106 = (bf16[4,3,64,128]{3,2,1,0:T(8,128)(2,1)}, bf16[4,3,64,128]{3,2,1,0:T(8,128)(2,1)S(1)}, u32[]{:S(2)}, u32[]{:S(2)}) collective-permute-start(bf16[4,3,64,128]{3,2,1,0:T(8,128)(2,1)} %get-tuple-element.212), channel_id=1, source_target_pairs={{0,24},{1,25},{2,26},{3,27},{4,28},{5,29},{6,30},{7,31},{8,16},{9,... | collective-permute-start | bytes 589832 | tf_op jit(solution)/shard_map/cond/branch_3_fun/ppermute | solution.py:310
  120.8 31.5 %collective-permute-start.107 = (bf16[4,3,64,128]{3,2,1,0:T(8,128)(2,1)}, bf16[4,3,64,128]{3,2,1,0:T(8,128)(2,1)S(1)}, u32[]{:S(2)}, u32[]{:S(2)}) collective-permute-start(bf16[4,3,64,128]{3,2,1,0:T(8,128)(2,1)} %get-tuple-element.213), channel_id=1, source_target_pairs={{0,28},{1,29},{2,30},{3,31},{4,24},{5,25},{6,26},{7,27},{8,20},{9,... | collective-permute-start | bytes 589832 | tf_op jit(solution)/shard_map/cond/branch_3_fun/ppermute | solution.py:310
  156.8 4.5 %collective-permute-start.122 = (bf16[16,3,64,128]{3,2,1,0:T(8,128)(2,1)}, bf16[16,3,64,128]{3,2,1,0:T(8,128)(2,1)}, u32[]{:S(2)}, u32[]{:S(2)}) collective-permute-start(bf16[16,3,64,128]{3,2,1,0:T(8,128)(2,1)} %get-tuple-element.232), channel_id=1, source_target_pairs={{0,1},{1,0},{2,3},{3,2},{4,5},{5,4},{6,7},{7,6},{8,9},{9,8},{10,11... | collective-permute-start | bytes 2359304 | tf_op jit(solution)/shard_map/cond/branch_3_fun/ppermute | solution.py:310
  158.5 3.4 %collective-permute-start.123 = (bf16[16,3,64,128]{3,2,1,0:T(8,128)(2,1)}, bf16[16,3,64,128]{3,2,1,0:T(8,128)(2,1)}, u32[]{:S(2)}, u32[]{:S(2)}) collective-permute-start(bf16[16,3,64,128]{3,2,1,0:T(8,128)(2,1)} %get-tuple-element.233), channel_id=1, source_target_pairs={{0,1},{1,0},{2,3},{3,2},{4,5},{5,4},{6,7},{7,6},{8,9},{9,8},{10,11... | collective-permute-start | bytes 2359304 | tf_op jit(solution)/shard_map/cond/branch_3_fun/ppermute | solution.py:310
  (31 other events, 978.9 us)
where the time goes:
time: 169 us; the launch traced here: 168 us
  waiting for transfers between devices  78.6 us (47%)
  starting transfers between devices  53.4 us (32%)
  Pallas kernels  33.1 us (20%)
    ppermute x31, waiting for transfers between devices, permute(): return lax.ppermute(value, ('gz', 'ky'), pairs)  78.6 us
    ppermute x31, starting transfers between devices, permute(): return lax.ppermute(value, ('gz', 'ky'), pairs)  53.4 us
    pallas_call x2, Pallas kernels, wall_rows(): pl.pallas_call(body, grid_spec=pltpu.PrefetchScalarGridSpec(num_scalar_pr...  9.73 us
    pallas_call x2, Pallas kernels, transform(): pl.pallas_call(body, grid_spec=pltpu.PrefetchScalarGridSpec(num_scalar_pr...  9.25 us
    pallas_call x2, Pallas kernels, windows(): pl.pallas_call(body, grid_spec=pltpu.PrefetchScalarGridSpec(num_scalar_pr...  6.62 us
    pallas_call x1, Pallas kernels, place_rows(): pl.pallas_call(body, grid_spec=pltpu.PrefetchScalarGridSpec(num_scalar_pr...  6.33 us
  transfers between devices with their start and end apart: 31, of which 15 were waited for; matrix products, arithmetic and copies ran while one was open for 0% of the time, Pallas kernels for 10%

commit v1 on v0

--- a/solution.py
+++ b/solution.py
@@ -56,12 +56,14 @@
             for group in range(4):
                 most = jnp.maximum(most, sent_runs(count_ref, group, flip)[1])
             choice = choice * len(sizes) + sum((most > size).astype(jnp.int32) for size in sizes[:-1])
-        out_ref[0] = choice
+        out_ref[0] = lax.axis_index("gz")
+        out_ref[1] = lax.axis_index("ky")
+        out_ref[2] = choice
 
     smem = pl.BlockSpec(memory_space=pltpu.SMEM)
     return pl.pallas_call(
-        body, in_specs=[smem], out_specs=smem, out_shape=jax.ShapeDtypeStruct((1,), jnp.int32)
-    )(count)[0]
+        body, in_specs=[smem], out_specs=smem, out_shape=jax.ShapeDtypeStruct((3,), jnp.int32)
+    )(count)
 
 
 def hbm_spec():
@@ -344,15 +346,15 @@
     factors = jnp.asarray(mode_factors(half_z))
     width = wall_operator.shape[0]
     rows_dev = fields.shape[3] // width
-    me = jnp.stack([lax.axis_index("gz"), lax.axis_index("ky")]).astype(jnp.int32)
+    sizes = [size for size in (12, 16) if 2 * size % devices == 0]
+    me = choose(remap_count, sizes)
     tables = (me, remap_offset, remap_count)
-    sizes = [size for size in (12, 16) if 2 * size % devices == 0]
     branches = [functools.partial(run, (far, near)) for far in sizes for near in sizes]
     arguments = (tables, fields, wall_operator, matrix, factors)
     if len(branches) == 1:
         held = branches[0](*arguments)
     else:
-        held = lax.switch(choose(remap_count, sizes), branches, *arguments)
+        held = lax.switch(me[2], branches, *arguments)
     return place_rows(me, remap_count, held, rows_dev, width)
 
 

time: 169 us -> 169 us (level)
  no operation moved by 1% of the time
where the time goes in v1:
time: 169 us
  waiting for transfers between devices  78.6 us (47%)
  starting transfers between devices  53.5 us (32%)
  Pallas kernels  33.2 us (20%)
  local copies, waits for them, and re-layouts  1.88 us (1%)
    ppermute x31, waiting for transfers between devices, permute(): return lax.ppermute(value, ('gz', 'ky'), pairs)  78.6 us
    ppermute x31, starting transfers between devices, permute(): return lax.ppermute(value, ('gz', 'ky'), pairs)  53.5 us
    pallas_call x2, Pallas kernels, wall_rows(): pl.pallas_call(body, grid_spec=pltpu.PrefetchScalarGridSpec(num_scalar_pr...  9.74 us
    pallas_call x2, Pallas kernels, transform(): pl.pallas_call(body, grid_spec=pltpu.PrefetchScalarGridSpec(num_scalar_pr...  9.24 us
    pallas_call x2, Pallas kernels, windows(): pl.pallas_call(body, grid_spec=pltpu.PrefetchScalarGridSpec(num_scalar_pr...  6.62 us
    pallas_call x1, Pallas kernels, place_rows(): pl.pallas_call(body, grid_spec=pltpu.PrefetchScalarGridSpec(num_scalar_pr...  6.33 us
  transfers between devices with their start and end apart: 31, of which 15 were waited for; matrix products, arithmetic and copies ran while one was open for 0% of the time, Pallas kernels for 10%

profile of v1, /device:TPU:17, one launch (start us, length us, event | category | flops | bytes accessed | tf_op | source)
XLA Modules:
  0.0 169.0 jit_solution(3678087784265687392)
XLA Ops:
  0.0 1.3 shard_map.64.me_ref
  2.5 159.9 %conditional.1 = (bf16[16,3,64,128]{3,2,1,0:T(8,128)(2,1)S(1)}, bf16[16,3,64,128]{3,2,1,0:T(8,128)(2,1)S(1)}, bf16[16,3,64,128]{3,2,1,0:T(8,128)(2,1)}, bf16[16,3,64,128]{3,2,1,0:T(8,128)(2,1)}) conditional(s32[]{:T(128)} %bitcast, (s32[3]{0:T(128)S(1)}, s32[4,4]{1,0:T(4,128)}, s32[4,4]{1,0:T(4,128)}, ...), branch_computations={%region_0.0_spmd, %region_1.0_spmd, %region_2.0_spmd, %region_3.0_... | conditional | flops 2415919104 | bytes 80218488 | solution.py:357
  3.1 4.9 %branch_3_fun.8 = (bf16[4,3,64,128]{3,2,1,0:T(8,128)(2,1)}, bf16[4,3,64,128]{3,2,1,0:T(8,128)(2,1)}, bf16[4,3,64,128]{3,2,1,0:T(8,128)(2,1)}, bf16[4,3,64,128]{3...) custom-call(s32[3]{0:T(128)S(1)} %get-tuple-element.191.me_ref, ...), custom_call_target="tpu_custom_call" | custom-call | flops 402653184 | bytes 4718592 | tf_op jit(solution)/shard_map/cond/branch_3_fun/pallas_call | solution.py:111
  10.7 3.3 %collective-permute-start.112 = (bf16[4,3,64,128]{3,2,1,0:T(8,128)(2,1)}, bf16[4,3,64,128]{3,2,1,0:T(8,128)(2,1)S(1)}, u32[]{:S(2)}, u32[]{:S(2)}) collective-permute-start(bf16[4,3,64,128]{3,2,1,0:T(8,128)(2,1)} %get-tuple-element.219), channel_id=1, source_target_pairs={{0,20},{1,21},{2,22},{3,23},{4,16},{5,17},{6,18},{7,19},{8,28},{9,... | collective-permute-start | bytes 589832 | tf_op jit(solution)/shard_map/cond/branch_3_fun/ppermute | solution.py:312
  14.0 4.8 %branch_3_fun.6 = (bf16[4,3,64,128]{3,2,1,0:T(8,128)(2,1)}, bf16[4,3,64,128]{3,2,1,0:T(8,128)(2,1)}, bf16[4,3,64,128]{3,2,1,0:T(8,128)(2,1)}, bf16[4,3,64,128]{3...) custom-call(s32[3]{0:T(128)S(1)} %get-tuple-element.191.me_ref, ...), custom_call_target="tpu_custom_call" | custom-call | flops 402653184 | bytes 4718592 | tf_op jit(solution)/shard_map/cond/branch_3_fun/pallas_call | solution.py:111
  20.3 4.0 %collective-permute-done.110.refs_3_ = bf16[4,3,64,128]{3,2,1,0:T(8,128)(2,1)S(1)} collective-permute-done((bf16[4,3,64,128]{3,2,1,0:T(8,128)(2,1)}, bf16[4,3,64,128]{3,2,1,0:T(8,128)(2,1)S(1)}, u32[]{:S(2)}, u32[]{:S(2)}) %collective-permute-start.110) | collective-permute-done | bytes 196640 | tf_op jit(solution)/shard_map/cond/branch_3_fun/ppermute | solution.py:312
  25.6 1.9 %collective-permute-done.112.refs_5_ = bf16[4,3,64,128]{3,2,1,0:T(8,128)(2,1)S(1)} collective-permute-done((bf16[4,3,64,128]{3,2,1,0:T(8,128)(2,1)}, bf16[4,3,64,128]{3,2,1,0:T(8,128)(2,1)S(1)}, u32[]{:S(2)}, u32[]{:S(2)}) %collective-permute-start.112) | collective-permute-done | bytes 196640 | tf_op jit(solution)/shard_map/cond/branch_3_fun/ppermute | solution.py:312
  27.4 13.7 %collective-permute-start.95 = (bf16[4,3,64,128]{3,2,1,0:T(8,128)(2,1)}, bf16[4,3,64,128]{3,2,1,0:T(8,128)(2,1)S(1)}, u32[]{:S(2)}, u32[]{:S(2)}) collective-permute-start(bf16[4,3,64,128]{3,2,1,0:T(8,128)(2,1)} %get-tuple-element.198), channel_id=1, source_target_pairs={{0,10},{1,11},{2,8},{3,9},{4,14},{5,15},{6,12},{7,13},{8,2},{9,3},... | collective-permute-start | bytes 589832 | tf_op jit(solution)/shard_map/cond/branch_3_fun/ppermute | solution.py:312
  42.2 5.3 %collective-permute-done.114.refs_7_ = bf16[4,3,64,128]{3,2,1,0:T(8,128)(2,1)S(1)} collective-permute-done((bf16[4,3,64,128]{3,2,1,0:T(8,128)(2,1)}, bf16[4,3,64,128]{3,2,1,0:T(8,128)(2,1)S(1)}, u32[]{:S(2)}, u32[]{:S(2)}) %collective-permute-start.114) | collective-permute-done | bytes 196640 | tf_op jit(solution)/shard_map/cond/branch_3_fun/ppermute | solution.py:312
  47.4 3.1 %collective-permute-start.98 = (bf16[4,3,64,128]{3,2,1,0:T(8,128)(2,1)}, bf16[4,3,64,128]{3,2,1,0:T(8,128)(2,1)S(1)}, u32[]{:S(2)}, u32[]{:S(2)}) collective-permute-start(bf16[4,3,64,128]{3,2,1,0:T(8,128)(2,1)} %get-tuple-element.201), channel_id=1, source_target_pairs={{0,22},{1,23},{2,20},{3,21},{4,18},{5,19},{6,16},{7,17},{8,30},{9,... | collective-permute-start | bytes 589832 | tf_op jit(solution)/shard_map/cond/branch_3_fun/ppermute | solution.py:312
  50.5 4.1 %collective-permute-start.99 = (bf16[4,3,64,128]{3,2,1,0:T(8,128)(2,1)}, bf16[4,3,64,128]{3,2,1,0:T(8,128)(2,1)S(1)}, u32[]{:S(2)}, u32[]{:S(2)}) collective-permute-start(bf16[4,3,64,128]{3,2,1,0:T(8,128)(2,1)} %get-tuple-element.202), channel_id=1, source_target_pairs={{0,26},{1,27},{2,24},{3,25},{4,30},{5,31},{6,28},{7,29},{8,18},{9,... | collective-permute-start | bytes 589832 | tf_op jit(solution)/shard_map/cond/branch_3_fun/ppermute | solution.py:312
  54.8 4.6 %branch_3_fun.9 = (bf16[4,3,64,128]{3,2,1,0:T(8,128)(2,1)}, bf16[4,3,64,128]{3,2,1,0:T(8,128)(2,1)}, bf16[4,3,64,128]{3,2,1,0:T(8,128)(2,1)}, bf16[4,3,64,128]{3...) custom-call(s32[3]{0:T(128)S(1)} %get-tuple-element.191.me_ref, ...), custom_call_target="tpu_custom_call" | custom-call | flops 805306368 | bytes 3145728 | tf_op jit(solution)/shard_map/cond/branch_3_fun/pallas_call | solution.py:161
  59.4 1.3 collective-permute-start.115
  60.7 2.1 %collective-permute-start.116 = (bf16[4,3,64,128]{3,2,1,0:T(8,128)(2,1)}, bf16[4,3,64,128]{3,2,1,0:T(8,128)(2,1)S(1)}, u32[]{:S(2)}, u32[]{:S(2)}) collective-permute-start(bf16[4,3,64,128]{3,2,1,0:T(8,128)(2,1)} %get-tuple-element.224), channel_id=1, source_target_pairs={{0,8},{1,9},{2,10},{3,11},{4,12},{5,13},{6,14},{7,15},{8,0},{9,1},... | collective-permute-start | bytes 589832 | tf_op jit(solution)/shard_map/cond/branch_3_fun/ppermute | solution.py:312
  62.8 9.1 %collective-permute-done.98.refs_5_ = bf16[4,3,64,128]{3,2,1,0:T(8,128)(2,1)S(1)} collective-permute-done((bf16[4,3,64,128]{3,2,1,0:T(8,128)(2,1)}, bf16[4,3,64,128]{3,2,1,0:T(8,128)(2,1)S(1)}, u32[]{:S(2)}, u32[]{:S(2)}) %collective-permute-start.98) | collective-permute-done | bytes 196640 | tf_op jit(solution)/shard_map/cond/branch_3_fun/ppermute | solution.py:312
  71.9 4.8 %collective-permute-start.117 = (bf16[4,3,64,128]{3,2,1,0:T(8,128)(2,1)}, bf16[4,3,64,128]{3,2,1,0:T(8,128)(2,1)S(1)}, u32[]{:S(2)}, u32[]{:S(2)}) collective-permute-start(bf16[4,3,64,128]{3,2,1,0:T(8,128)(2,1)} %get-tuple-element.225), channel_id=1, source_target_pairs={{0,12},{1,13},{2,14},{3,15},{4,8},{5,9},{6,10},{7,11},{8,4},{9,5},... | collective-permute-start | bytes 589832 | tf_op jit(solution)/shard_map/cond/branch_3_fun/ppermute | solution.py:312
  76.7 2.1 %collective-permute-done.99.refs_6_ = bf16[4,3,64,128]{3,2,1,0:T(8,128)(2,1)S(1)} collective-permute-done((bf16[4,3,64,128]{3,2,1,0:T(8,128)(2,1)}, bf16[4,3,64,128]{3,2,1,0:T(8,128)(2,1)S(1)}, u32[]{:S(2)}, u32[]{:S(2)}) %collective-permute-start.99) | collective-permute-done | bytes 196640 | tf_op jit(solution)/shard_map/cond/branch_3_fun/ppermute | solution.py:312
  78.8 7.6 %collective-permute-done.100.refs_7_ = bf16[4,3,64,128]{3,2,1,0:T(8,128)(2,1)S(1)} collective-permute-done((bf16[4,3,64,128]{3,2,1,0:T(8,128)(2,1)}, bf16[4,3,64,128]{3,2,1,0:T(8,128)(2,1)S(1)}, u32[]{:S(2)}, u32[]{:S(2)}) %collective-permute-start.100) | collective-permute-done | bytes 196640 | tf_op jit(solution)/shard_map/cond/branch_3_fun/ppermute | solution.py:312
  87.1 4.6 %branch_3_fun.7 = (bf16[4,3,64,128]{3,2,1,0:T(8,128)(2,1)}, bf16[4,3,64,128]{3,2,1,0:T(8,128)(2,1)}, bf16[4,3,64,128]{3,2,1,0:T(8,128)(2,1)}, bf16[4,3,64,128]{3...) custom-call(s32[3]{0:T(128)S(1)} %get-tuple-element.191.me_ref, ...), custom_call_target="tpu_custom_call" | custom-call | flops 805306368 | bytes 3145728 | tf_op jit(solution)/shard_map/cond/branch_3_fun/pallas_call | solution.py:161
  91.9 2.5 %collective-permute-start.101 = (bf16[4,3,64,128]{3,2,1,0:T(8,128)(2,1)}, bf16[4,3,64,128]{3,2,1,0:T(8,128)(2,1)S(1)}, u32[]{:S(2)}, u32[]{:S(2)}) collective-permute-start(bf16[4,3,64,128]{3,2,1,0:T(8,128)(2,1)} %get-tuple-element.207), channel_id=1, source_target_pairs={{0,4},{1,5},{2,6},{3,7},{4,0},{5,1},{6,2},{7,3},{8,12},{9,13},{10,... | collective-permute-start | bytes 589832 | tf_op jit(solution)/shard_map/cond/branch_3_fun/ppermute | solution.py:312
  94.4 2.1 %collective-permute-start.102 = (bf16[4,3,64,128]{3,2,1,0:T(8,128)(2,1)}, bf16[4,3,64,128]{3,2,1,0:T(8,128)(2,1)S(1)}, u32[]{:S(2)}, u32[]{:S(2)}) collective-permute-start(bf16[4,3,64,128]{3,2,1,0:T(8,128)(2,1)} %get-tuple-element.208), channel_id=1, source_target_pairs={{0,8},{1,9},{2,10},{3,11},{4,12},{5,13},{6,14},{7,15},{8,0},{9,1},... | collective-permute-start | bytes 589832 | tf_op jit(solution)/shard_map/cond/branch_3_fun/ppermute | solution.py:312
  97.2 9.0 %collective-permute-start.103 = (bf16[4,3,64,128]{3,2,1,0:T(8,128)(2,1)}, bf16[4,3,64,128]{3,2,1,0:T(8,128)(2,1)S(1)}, u32[]{:S(2)}, u32[]{:S(2)}) collective-permute-start(bf16[4,3,64,128]{3,2,1,0:T(8,128)(2,1)} %get-tuple-element.209), channel_id=1, source_target_pairs={{0,12},{1,13},{2,14},{3,15},{4,8},{5,9},{6,10},{7,11},{8,4},{9,5},... | collective-permute-start | bytes 589832 | tf_op jit(solution)/shard_map/cond/branch_3_fun/ppermute | solution.py:312
  106.2 6.3 %collective-permute-done.120.refs_14_ = bf16[4,3,64,128]{3,2,1,0:T(8,128)(2,1)S(1)} collective-permute-done((bf16[4,3,64,128]{3,2,1,0:T(8,128)(2,1)}, bf16[4,3,64,128]{3,2,1,0:T(8,128)(2,1)S(1)}, u32[]{:S(2)}, u32[]{:S(2)}) %collective-permute-start.120) | collective-permute-done | bytes 196640 | tf_op jit(solution)/shard_map/cond/branch_3_fun/ppermute | solution.py:312
  112.6 8.7 %collective-permute-done.121.refs_15_ = bf16[4,3,64,128]{3,2,1,0:T(8,128)(2,1)S(1)} collective-permute-done((bf16[4,3,64,128]{3,2,1,0:T(8,128)(2,1)}, bf16[4,3,64,128]{3,2,1,0:T(8,128)(2,1)S(1)}, u32[]{:S(2)}, u32[]{:S(2)}) %collective-permute-start.121) | collective-permute-done | bytes 196640 | tf_op jit(solution)/shard_map/cond/branch_3_fun/ppermute | solution.py:312
  121.5 7.3 %collective-permute-done.104.refs_4_ = bf16[4,3,64,128]{3,2,1,0:T(8,128)(2,1)S(1)} collective-permute-done((bf16[4,3,64,128]{3,2,1,0:T(8,128)(2,1)}, bf16[4,3,64,128]{3,2,1,0:T(8,128)(2,1)S(1)}, u32[]{:S(2)}, u32[]{:S(2)}) %collective-permute-start.104) | collective-permute-done | bytes 196640 | tf_op jit(solution)/shard_map/cond/branch_3_fun/ppermute | solution.py:312
  128.8 4.3 %collective-permute-done.105.refs_5_ = bf16[4,3,64,128]{3,2,1,0:T(8,128)(2,1)S(1)} collective-permute-done((bf16[4,3,64,128]{3,2,1,0:T(8,128)(2,1)}, bf16[4,3,64,128]{3,2,1,0:T(8,128)(2,1)S(1)}, u32[]{:S(2)}, u32[]{:S(2)}) %collective-permute-start.105) | collective-permute-done | bytes 196640 | tf_op jit(solution)/shard_map/cond/branch_3_fun/ppermute | solution.py:312
  133.1 13.2 %collective-permute-done.106.refs_6_ = bf16[4,3,64,128]{3,2,1,0:T(8,128)(2,1)S(1)} collective-permute-done((bf16[4,3,64,128]{3,2,1,0:T(8,128)(2,1)}, bf16[4,3,64,128]{3,2,1,0:T(8,128)(2,1)S(1)}, u32[]{:S(2)}, u32[]{:S(2)}) %collective-permute-start.106) | collective-permute-done | bytes 196640 | tf_op jit(solution)/shard_map/cond/branch_3_fun/ppermute | solution.py:312
  146.3 6.6 %collective-permute-done.107.refs_7_ = bf16[4,3,64,128]{3,2,1,0:T(8,128)(2,1)S(1)} collective-permute-done((bf16[4,3,64,128]{3,2,1,0:T(8,128)(2,1)}, bf16[4,3,64,128]{3,2,1,0:T(8,128)(2,1)S(1)}, u32[]{:S(2)}, u32[]{:S(2)}) %collective-permute-start.107) | collective-permute-done | bytes 196640 | tf_op jit(solution)/shard_map/cond/branch_3_fun/ppermute | solution.py:312
  153.5 3.9 %branch_3_fun.11 = (bf16[16,3,64,128]{3,2,1,0:T(8,128)(2,1)}, bf16[16,3,64,128]{3,2,1,0:T(8,128)(2,1)}) custom-call(s32[3]{0:T(128)S(1)} %get-tuple-element.191.me_ref, s32[4,4]{1,0:T(4,128)S(1)} %copy-done.24, bf16[4,3,64,128]{3,2,1,0:T(8,128)(2,1)} %get-tuple-element.206.refs_0_, bf16[4,3,64,128]{3,2,1,0:T(8,128)(2,1)} %copy-done.7, ...), custom_call_target="tpu_custom_call" | custom-call | bytes 4194304 | tf_op jit(solution)/shard_map/cond/branch_3_fun/pallas_call | solution.py:217
  157.4 1.6 collective-permute-start.122
  159.2 2.7 %branch_3_fun.10 = (bf16[16,3,64,128]{3,2,1,0:T(8,128)(2,1)S(1)}, bf16[16,3,64,128]{3,2,1,0:T(8,128)(2,1)S(1)}) custom-call(s32[3]{0:T(128)S(1)} %get-tuple-element.191.me_ref, s32[4,4]{1,0:T(4,128)S(1)} %copy-done.24, bf16[4,3,64,128]{3,2,1,0:T(8,128)(2,1)} %get-tuple-element.206.refs_0_, bf16[4,3,64,128]{3,2,1,0:T(8,128)(2,1)} %copy-done.7, ...), custom_call_target="tpu_custom_call" | custom-call | bytes 4194304 | tf_op jit(solution)/shard_map/cond/branch_3_fun/pallas_call | solution.py:217
  162.5 6.3 %shard_map.65 = f32[32,3,2,8192]{3,2,1,0:T(2,128)} custom-call(s32[3]{0:T(128)S(1)} %shard_map.64.me_ref, s32[4,4]{1,0:T(4,128)} %count_ref.3, bf16[16,3,64,128]{3,2,1,0:T(8,128)(2,1)S(1)} %get-tuple-element.238.refs_0_, bf16[16,3,64,128]{3,2,1,0:T(8,128)(2,1)S(1)} %get-tuple-element.239.refs_1_, bf16[16,3,64,128]{3,2,1,0:T(8,128)(2,1)} %get-tuple-element.240.refs_2_, ...), custom_call_target="tpu_custom_call" | custom-call | bytes 9437184 | tf_op jit(solution)/shard_map/pallas_call | solution.py:284
  (104 shorter events, 9.9 us)
Async XLA Ops:
  3.1 150.5 %copy-start.24 = (s32[4,4]{1,0:T(4,128)S(1)}, s32[4,4]{1,0:T(4,128)}, u32[]{:S(2)}) copy-start(s32[4,4]{1,0:T(4,128)} %get-tuple-element.192.count_ref) | copy-start | bytes 196 | tf_op jit(solution)/shard_map/cond
  8.0 10.8 %collective-permute-start.108 = (bf16[4,3,64,128]{3,2,1,0:T(8,128)(2,1)}, bf16[4,3,64,128]{3,2,1,0:T(8,128)(2,1)S(1)}, u32[]{:S(2)}, u32[]{:S(2)}) collective-permute-start(bf16[4,3,64,128]{3,2,1,0:T(8,128)(2,1)} %get-tuple-element.215), channel_id=1, source_target_pairs={{0,4},{1,5},{2,6},{3,7},{4,0},{5,1},{6,2},{7,3},{8,12},{9,13},{10,... | collective-permute-start | bytes 589832 | tf_op jit(solution)/shard_map/cond/branch_3_fun/ppermute | solution.py:312
  9.3 9.8 %collective-permute-start.109 = (bf16[4,3,64,128]{3,2,1,0:T(8,128)(2,1)}, bf16[4,3,64,128]{3,2,1,0:T(8,128)(2,1)S(1)}, u32[]{:S(2)}, u32[]{:S(2)}) collective-permute-start(bf16[4,3,64,128]{3,2,1,0:T(8,128)(2,1)} %get-tuple-element.216), channel_id=1, source_target_pairs={{0,8},{1,9},{2,10},{3,11},{4,12},{5,13},{6,14},{7,15},{8,0},{9,1},... | collective-permute-start | bytes 589832 | tf_op jit(solution)/shard_map/cond/branch_3_fun/ppermute | solution.py:312
  10.6 13.7 %collective-permute-start.110 = (bf16[4,3,64,128]{3,2,1,0:T(8,128)(2,1)}, bf16[4,3,64,128]{3,2,1,0:T(8,128)(2,1)S(1)}, u32[]{:S(2)}, u32[]{:S(2)}) collective-permute-start(bf16[4,3,64,128]{3,2,1,0:T(8,128)(2,1)} %get-tuple-element.217), channel_id=1, source_target_pairs={{0,12},{1,13},{2,14},{3,15},{4,8},{5,9},{6,10},{7,11},{8,4},{9,5},... | collective-permute-start | bytes 589832 | tf_op jit(solution)/shard_map/cond/branch_3_fun/ppermute | solution.py:312
  10.7 14.9 %collective-permute-start.111 = (bf16[4,3,64,128]{3,2,1,0:T(8,128)(2,1)}, bf16[4,3,64,128]{3,2,1,0:T(8,128)(2,1)S(1)}, u32[]{:S(2)}, u32[]{:S(2)}) collective-permute-start(bf16[4,3,64,128]{3,2,1,0:T(8,128)(2,1)} %get-tuple-element.218), channel_id=1, source_target_pairs={{0,16},{1,17},{2,18},{3,19},{4,20},{5,21},{6,22},{7,23},{8,24},{9,... | collective-permute-start | bytes 589832 | tf_op jit(solution)/shard_map/cond/branch_3_fun/ppermute | solution.py:312
  10.7 16.8 %collective-permute-start.112 = (bf16[4,3,64,128]{3,2,1,0:T(8,128)(2,1)}, bf16[4,3,64,128]{3,2,1,0:T(8,128)(2,1)S(1)}, u32[]{:S(2)}, u32[]{:S(2)}) collective-permute-start(bf16[4,3,64,128]{3,2,1,0:T(8,128)(2,1)} %get-tuple-element.219), channel_id=1, source_target_pairs={{0,20},{1,21},{2,22},{3,23},{4,16},{5,17},{6,18},{7,19},{8,28},{9,... | collective-permute-start | bytes 589832 | tf_op jit(solution)/shard_map/cond/branch_3_fun/ppermute | solution.py:312
  18.8 23.3 %collective-permute-start.113 = (bf16[4,3,64,128]{3,2,1,0:T(8,128)(2,1)}, bf16[4,3,64,128]{3,2,1,0:T(8,128)(2,1)S(1)}, u32[]{:S(2)}, u32[]{:S(2)}) collective-permute-start(bf16[4,3,64,128]{3,2,1,0:T(8,128)(2,1)} %get-tuple-element.220), channel_id=1, source_target_pairs={{0,24},{1,25},{2,26},{3,27},{4,28},{5,29},{6,30},{7,31},{8,16},{9,... | collective-permute-start | bytes 589832 | tf_op jit(solution)/shard_map/cond/branch_3_fun/ppermute | solution.py:312
  19.0 28.4 %collective-permute-start.114 = (bf16[4,3,64,128]{3,2,1,0:T(8,128)(2,1)}, bf16[4,3,64,128]{3,2,1,0:T(8,128)(2,1)S(1)}, u32[]{:S(2)}, u32[]{:S(2)}) collective-permute-start(bf16[4,3,64,128]{3,2,1,0:T(8,128)(2,1)} %get-tuple-element.221), channel_id=1, source_target_pairs={{0,28},{1,29},{2,30},{3,31},{4,24},{5,25},{6,26},{7,27},{8,20},{9,... | collective-permute-start | bytes 589832 | tf_op jit(solution)/shard_map/cond/branch_3_fun/ppermute | solution.py:312
  24.3 23.1 %collective-permute-start.93 = (bf16[4,3,64,128]{3,2,1,0:T(8,128)(2,1)}, bf16[4,3,64,128]{3,2,1,0:T(8,128)(2,1)S(1)}, u32[]{:S(2)}, u32[]{:S(2)}) collective-permute-start(bf16[4,3,64,128]{3,2,1,0:T(8,128)(2,1)} %get-tuple-element.196), channel_id=1, source_target_pairs={{0,2},{1,3},{2,0},{3,1},{4,6},{5,7},{6,4},{7,5},{8,10},{9,11},{10,... | collective-permute-start | bytes 589832 | tf_op jit(solution)/shard_map/cond/branch_3_fun/ppermute | solution.py:312
  25.5 25.0 %collective-permute-start.94 = (bf16[4,3,64,128]{3,2,1,0:T(8,128)(2,1)}, bf16[4,3,64,128]{3,2,1,0:T(8,128)(2,1)S(1)}, u32[]{:S(2)}, u32[]{:S(2)}) collective-permute-start(bf16[4,3,64,128]{3,2,1,0:T(8,128)(2,1)} %get-tuple-element.197), channel_id=1, source_target_pairs={{0,6},{1,7},{2,4},{3,5},{4,2},{5,3},{6,0},{7,1},{8,14},{9,15},{10,... | collective-permute-start | bytes 589832 | tf_op jit(solution)/shard_map/cond/branch_3_fun/ppermute | solution.py:312
  27.4 27.2 %collective-permute-start.95 = (bf16[4,3,64,128]{3,2,1,0:T(8,128)(2,1)}, bf16[4,3,64,128]{3,2,1,0:T(8,128)(2,1)S(1)}, u32[]{:S(2)}, u32[]{:S(2)}) collective-permute-start(bf16[4,3,64,128]{3,2,1,0:T(8,128)(2,1)} %get-tuple-element.198), channel_id=1, source_target_pairs={{0,10},{1,11},{2,8},{3,9},{4,14},{5,15},{6,12},{7,13},{8,2},{9,3},... | collective-permute-start | bytes 589832 | tf_op jit(solution)/shard_map/cond/branch_3_fun/ppermute | solution.py:312
  42.2 17.3 %collective-permute-start.96 = (bf16[4,3,64,128]{3,2,1,0:T(8,128)(2,1)}, bf16[4,3,64,128]{3,2,1,0:T(8,128)(2,1)S(1)}, u32[]{:S(2)}, u32[]{:S(2)}) collective-permute-start(bf16[4,3,64,128]{3,2,1,0:T(8,128)(2,1)} %get-tuple-element.199), channel_id=1, source_target_pairs={{0,14},{1,15},{2,12},{3,13},{4,10},{5,11},{6,8},{7,9},{8,6},{9,7},... | collective-permute-start | bytes 589832 | tf_op jit(solution)/shard_map/cond/branch_3_fun/ppermute | solution.py:312
  47.4 13.3 %collective-permute-start.97 = (bf16[4,3,64,128]{3,2,1,0:T(8,128)(2,1)}, bf16[4,3,64,128]{3,2,1,0:T(8,128)(2,1)S(1)}, u32[]{:S(2)}, u32[]{:S(2)}) collective-permute-start(bf16[4,3,64,128]{3,2,1,0:T(8,128)(2,1)} %get-tuple-element.200), channel_id=1, source_target_pairs={{0,18},{1,19},{2,16},{3,17},{4,22},{5,23},{6,20},{7,21},{8,26},{9,... | collective-permute-start | bytes 589832 | tf_op jit(solution)/shard_map/cond/branch_3_fun/ppermute | solution.py:312
  47.4 24.5 %collective-permute-start.98 = (bf16[4,3,64,128]{3,2,1,0:T(8,128)(2,1)}, bf16[4,3,64,128]{3,2,1,0:T(8,128)(2,1)S(1)}, u32[]{:S(2)}, u32[]{:S(2)}) collective-permute-start(bf16[4,3,64,128]{3,2,1,0:T(8,128)(2,1)} %get-tuple-element.201), channel_id=1, source_target_pairs={{0,22},{1,23},{2,20},{3,21},{4,18},{5,19},{6,16},{7,17},{8,30},{9,... | collective-permute-start | bytes 589832 | tf_op jit(solution)/shard_map/cond/branch_3_fun/ppermute | solution.py:312
  50.5 28.3 %collective-permute-start.99 = (bf16[4,3,64,128]{3,2,1,0:T(8,128)(2,1)}, bf16[4,3,64,128]{3,2,1,0:T(8,128)(2,1)S(1)}, u32[]{:S(2)}, u32[]{:S(2)}) collective-permute-start(bf16[4,3,64,128]{3,2,1,0:T(8,128)(2,1)} %get-tuple-element.202), channel_id=1, source_target_pairs={{0,26},{1,27},{2,24},{3,25},{4,30},{5,31},{6,28},{7,29},{8,18},{9,... | collective-permute-start | bytes 589832 | tf_op jit(solution)/shard_map/cond/branch_3_fun/ppermute | solution.py:312
  54.7 31.7 %collective-permute-start.100 = (bf16[4,3,64,128]{3,2,1,0:T(8,128)(2,1)}, bf16[4,3,64,128]{3,2,1,0:T(8,128)(2,1)S(1)}, u32[]{:S(2)}, u32[]{:S(2)}) collective-permute-start(bf16[4,3,64,128]{3,2,1,0:T(8,128)(2,1)} %get-tuple-element.203), channel_id=1, source_target_pairs={{0,30},{1,31},{2,28},{3,29},{4,26},{5,27},{6,24},{7,25},{8,22},{9,... | collective-permute-start | bytes 589832 | tf_op jit(solution)/shard_map/cond/branch_3_fun/ppermute | solution.py:312
  59.4 32.3 %collective-permute-start.115 = (bf16[4,3,64,128]{3,2,1,0:T(8,128)(2,1)}, bf16[4,3,64,128]{3,2,1,0:T(8,128)(2,1)S(1)}, u32[]{:S(2)}, u32[]{:S(2)}) collective-permute-start(bf16[4,3,64,128]{3,2,1,0:T(8,128)(2,1)} %get-tuple-element.223), channel_id=1, source_target_pairs={{0,4},{1,5},{2,6},{3,7},{4,0},{5,1},{6,2},{7,3},{8,12},{9,13},{10,... | collective-permute-start | bytes 589832 | tf_op jit(solution)/shard_map/cond/branch_3_fun/ppermute | solution.py:312
  60.7 31.0 %collective-permute-start.116 = (bf16[4,3,64,128]{3,2,1,0:T(8,128)(2,1)}, bf16[4,3,64,128]{3,2,1,0:T(8,128)(2,1)S(1)}, u32[]{:S(2)}, u32[]{:S(2)}) collective-permute-start(bf16[4,3,64,128]{3,2,1,0:T(8,128)(2,1)} %get-tuple-element.224), channel_id=1, source_target_pairs={{0,8},{1,9},{2,10},{3,11},{4,12},{5,13},{6,14},{7,15},{8,0},{9,1},... | collective-permute-start | bytes 589832 | tf_op jit(solution)/shard_map/cond/branch_3_fun/ppermute | solution.py:312
  71.9 20.0 %collective-permute-start.117 = (bf16[4,3,64,128]{3,2,1,0:T(8,128)(2,1)}, bf16[4,3,64,128]{3,2,1,0:T(8,128)(2,1)S(1)}, u32[]{:S(2)}, u32[]{:S(2)}) collective-permute-start(bf16[4,3,64,128]{3,2,1,0:T(8,128)(2,1)} %get-tuple-element.225), channel_id=1, source_target_pairs={{0,12},{1,13},{2,14},{3,15},{4,8},{5,9},{6,10},{7,11},{8,4},{9,5},... | collective-permute-start | bytes 589832 | tf_op jit(solution)/shard_map/cond/branch_3_fun/ppermute | solution.py:312
  78.8 15.6 %collective-permute-start.118 = (bf16[4,3,64,128]{3,2,1,0:T(8,128)(2,1)}, bf16[4,3,64,128]{3,2,1,0:T(8,128)(2,1)S(1)}, u32[]{:S(2)}, u32[]{:S(2)}) collective-permute-start(bf16[4,3,64,128]{3,2,1,0:T(8,128)(2,1)} %get-tuple-element.226), channel_id=1, source_target_pairs={{0,16},{1,17},{2,18},{3,19},{4,20},{5,21},{6,22},{7,23},{8,24},{9,... | collective-permute-start | bytes 589832 | tf_op jit(solution)/shard_map/cond/branch_3_fun/ppermute | solution.py:312
  86.4 10.8 %collective-permute-start.119 = (bf16[4,3,64,128]{3,2,1,0:T(8,128)(2,1)}, bf16[4,3,64,128]{3,2,1,0:T(8,128)(2,1)S(1)}, u32[]{:S(2)}, u32[]{:S(2)}) collective-permute-start(bf16[4,3,64,128]{3,2,1,0:T(8,128)(2,1)} %get-tuple-element.227), channel_id=1, source_target_pairs={{0,20},{1,21},{2,22},{3,23},{4,16},{5,17},{6,18},{7,19},{8,28},{9,... | collective-permute-start | bytes 589832 | tf_op jit(solution)/shard_map/cond/branch_3_fun/ppermute | solution.py:312
  91.7 20.9 %collective-permute-start.120 = (bf16[4,3,64,128]{3,2,1,0:T(8,128)(2,1)}, bf16[4,3,64,128]{3,2,1,0:T(8,128)(2,1)S(1)}, u32[]{:S(2)}, u32[]{:S(2)}) collective-permute-start(bf16[4,3,64,128]{3,2,1,0:T(8,128)(2,1)} %get-tuple-element.228), channel_id=1, source_target_pairs={{0,24},{1,25},{2,26},{3,27},{4,28},{5,29},{6,30},{7,31},{8,16},{9,... | collective-permute-start | bytes 589832 | tf_op jit(solution)/shard_map/cond/branch_3_fun/ppermute | solution.py:312
  91.8 29.5 %collective-permute-start.121 = (bf16[4,3,64,128]{3,2,1,0:T(8,128)(2,1)}, bf16[4,3,64,128]{3,2,1,0:T(8,128)(2,1)S(1)}, u32[]{:S(2)}, u32[]{:S(2)}) collective-permute-start(bf16[4,3,64,128]{3,2,1,0:T(8,128)(2,1)} %get-tuple-element.229), channel_id=1, source_target_pairs={{0,28},{1,29},{2,30},{3,31},{4,24},{5,25},{6,26},{7,27},{8,20},{9,... | collective-permute-start | bytes 589832 | tf_op jit(solution)/shard_map/cond/branch_3_fun/ppermute | solution.py:312
  91.9 29.4 %collective-permute-start.101 = (bf16[4,3,64,128]{3,2,1,0:T(8,128)(2,1)}, bf16[4,3,64,128]{3,2,1,0:T(8,128)(2,1)S(1)}, u32[]{:S(2)}, u32[]{:S(2)}) collective-permute-start(bf16[4,3,64,128]{3,2,1,0:T(8,128)(2,1)} %get-tuple-element.207), channel_id=1, source_target_pairs={{0,4},{1,5},{2,6},{3,7},{4,0},{5,1},{6,2},{7,3},{8,12},{9,13},{10,... | collective-permute-start | bytes 589832 | tf_op jit(solution)/shard_map/cond/branch_3_fun/ppermute | solution.py:312
  94.4 26.9 %collective-permute-start.102 = (bf16[4,3,64,128]{3,2,1,0:T(8,128)(2,1)}, bf16[4,3,64,128]{3,2,1,0:T(8,128)(2,1)S(1)}, u32[]{:S(2)}, u32[]{:S(2)}) collective-permute-start(bf16[4,3,64,128]{3,2,1,0:T(8,128)(2,1)} %get-tuple-element.208), channel_id=1, source_target_pairs={{0,8},{1,9},{2,10},{3,11},{4,12},{5,13},{6,14},{7,15},{8,0},{9,1},... | collective-permute-start | bytes 589832 | tf_op jit(solution)/shard_map/cond/branch_3_fun/ppermute | solution.py:312
  97.2 24.3 %collective-permute-start.103 = (bf16[4,3,64,128]{3,2,1,0:T(8,128)(2,1)}, bf16[4,3,64,128]{3,2,1,0:T(8,128)(2,1)S(1)}, u32[]{:S(2)}, u32[]{:S(2)}) collective-permute-start(bf16[4,3,64,128]{3,2,1,0:T(8,128)(2,1)} %get-tuple-element.209), channel_id=1, source_target_pairs={{0,12},{1,13},{2,14},{3,15},{4,8},{5,9},{6,10},{7,11},{8,4},{9,5},... | collective-permute-start | bytes 589832 | tf_op jit(solution)/shard_map/cond/branch_3_fun/ppermute | solution.py:312
  112.6 16.2 %collective-permute-start.104 = (bf16[4,3,64,128]{3,2,1,0:T(8,128)(2,1)}, bf16[4,3,64,128]{3,2,1,0:T(8,128)(2,1)S(1)}, u32[]{:S(2)}, u32[]{:S(2)}) collective-permute-start(bf16[4,3,64,128]{3,2,1,0:T(8,128)(2,1)} %get-tuple-element.210), channel_id=1, source_target_pairs={{0,16},{1,17},{2,18},{3,19},{4,20},{5,21},{6,22},{7,23},{8,24},{9,... | collective-permute-start | bytes 589832 | tf_op jit(solution)/shard_map/cond/branch_3_fun/ppermute | solution.py:312
  121.3 11.8 %collective-permute-start.105 = (bf16[4,3,64,128]{3,2,1,0:T(8,128)(2,1)}, bf16[4,3,64,128]{3,2,1,0:T(8,128)(2,1)S(1)}, u32[]{:S(2)}, u32[]{:S(2)}) collective-permute-start(bf16[4,3,64,128]{3,2,1,0:T(8,128)(2,1)} %get-tuple-element.211), channel_id=1, source_target_pairs={{0,20},{1,21},{2,22},{3,23},{4,16},{5,17},{6,18},{7,19},{8,28},{9,... | collective-permute-start | bytes 589832 | tf_op jit(solution)/shard_map/cond/branch_3_fun/ppermute | solution.py:312
  121.3 25.0 %collective-permute-start.106 = (bf16[4,3,64,128]{3,2,1,0:T(8,128)(2,1)}, bf16[4,3,64,128]{3,2,1,0:T(8,128)(2,1)S(1)}, u32[]{:S(2)}, u32[]{:S(2)}) collective-permute-start(bf16[4,3,64,128]{3,2,1,0:T(8,128)(2,1)} %get-tuple-element.212), channel_id=1, source_target_pairs={{0,24},{1,25},{2,26},{3,27},{4,28},{5,29},{6,30},{7,31},{8,16},{9,... | collective-permute-start | bytes 589832 | tf_op jit(solution)/shard_map/cond/branch_3_fun/ppermute | solution.py:312
  121.4 31.5 %collective-permute-start.107 = (bf16[4,3,64,128]{3,2,1,0:T(8,128)(2,1)}, bf16[4,3,64,128]{3,2,1,0:T(8,128)(2,1)S(1)}, u32[]{:S(2)}, u32[]{:S(2)}) collective-permute-start(bf16[4,3,64,128]{3,2,1,0:T(8,128)(2,1)} %get-tuple-element.213), channel_id=1, source_target_pairs={{0,28},{1,29},{2,30},{3,31},{4,24},{5,25},{6,26},{7,27},{8,20},{9,... | collective-permute-start | bytes 589832 | tf_op jit(solution)/shard_map/cond/branch_3_fun/ppermute | solution.py:312
  157.4 4.5 %collective-permute-start.122 = (bf16[16,3,64,128]{3,2,1,0:T(8,128)(2,1)}, bf16[16,3,64,128]{3,2,1,0:T(8,128)(2,1)}, u32[]{:S(2)}, u32[]{:S(2)}) collective-permute-start(bf16[16,3,64,128]{3,2,1,0:T(8,128)(2,1)} %get-tuple-element.232), channel_id=1, source_target_pairs={{0,1},{1,0},{2,3},{3,2},{4,5},{5,4},{6,7},{7,6},{8,9},{9,8},{10,11... | collective-permute-start | bytes 2359304 | tf_op jit(solution)/shard_map/cond/branch_3_fun/ppermute | solution.py:312
  159.1 3.4 %collective-permute-start.123 = (bf16[16,3,64,128]{3,2,1,0:T(8,128)(2,1)}, bf16[16,3,64,128]{3,2,1,0:T(8,128)(2,1)}, u32[]{:S(2)}, u32[]{:S(2)}) collective-permute-start(bf16[16,3,64,128]{3,2,1,0:T(8,128)(2,1)} %get-tuple-element.233), channel_id=1, source_target_pairs={{0,1},{1,0},{2,3},{3,2},{4,5},{5,4},{6,7},{7,6},{8,9},{9,8},{10,11... | collective-permute-start | bytes 2359304 | tf_op jit(solution)/shard_map/cond/branch_3_fun/ppermute | solution.py:312
  (31 other events, 979.3 us)
